TPU v7x, 128 devices: a whole 4x4x4 slice. The times are simulated.
128 devices in a mesh: rep: 16 (over z_hi, x, core), tp: 8 (over z_lo, y).
Axes of the slice: x: 4, y: 4, z: 4 (z_hi: 2, z_lo: 2; z = z_hi * 2 + z_lo), core: 2. Of those that a mesh axis runs over, the one named last changes fastest.
Arguments:
- out_master: float32 [4096, 8192], P(None, ('rep', 'tp')), may hold values from -1 to 1
- out_base: bfloat16 [4096, 8192], P(None, ('rep', 'tp')), may hold values from -1 to 1
- out_held: bfloat16 [4096, 8192], P('tp'), may hold values from -1 to 1
- out_scales: int32 [32, 64], replicated, may hold values from -14 to -11, as said below
- query_master: float32 [8192, 4096], P(('rep', 'tp')), may hold values from -1 to 1
- query_base: bfloat16 [8192, 4096], P(('rep', 'tp')), may hold values from -1 to 1
- query_held: bfloat16 [8192, 4096], P(None, 'tp'), may hold values from -1 to 1
- query_scales: int32 [64, 32], replicated, may hold values from -14 to -11, as said below
- attention: bfloat16 [4, 2048, 4096], P(None, 'rep', 'tp'), may hold values from -6 to 6
- residual: bfloat16 [4, 2048, 8192], P(None, 'rep', 'tp'), may hold values from -100 to 100
- norm_gain: float32 [8192], P('tp'), may hold values from 0.25 to 1.75
Outputs:
- queries: bfloat16 [4, 2048, 4096], P(None, 'rep', 'tp')
Inputs may be any that keep to these rules, and one draw needn't show every extreme that they name: `out_scales`: the exponent of the power-of-two scale of each 128 x 128 block. `query_scales`: the exponent of the power-of-two scale of each 128 x 128 block.
All inputs are finite; a program needn't handle non-finite values.
Results may differ from a plain program's by a relative error of at most 0.017.
Values may be sent and summed in bfloat16 or wider, within the bound.
No kernel may reach another device: no remote copies, remote signals or barrier semaphores. Data moves between devices by JAX's collectives and lax.ppermute only.
A program may use at most 128 MiB of HBM per device.

v0:
```python
import functools

import jax
import jax.numpy as jnp
from jax import lax
from jax.experimental import pallas as pl
from jax.experimental.pallas import tpu as pltpu
from jax.sharding import PartitionSpec as P

BLOCK = 128
CHUNKS = 2
code_limit = 448.0
f32 = jnp.float32
bf16 = jnp.bfloat16
NT = (((1,), (1,)), ((), ()))
ANY = pl.BlockSpec(memory_space=pl.ANY)
LIMIT = pltpu.CompilerParams(vmem_limit_bytes=48 * 2**20)


def move_rep(v, dz=0, dx=0, dc=0):
    perm = []
    for r in range(16):
        z, x, c = r // 8, (r // 2) % 4, r % 2
        perm.append((r, (((z + dz) % 2) * 4 + (x + dx) % 4) * 2 + (c + dc) % 2))
    return lax.ppermute(v, "rep", perm)


def move_tp(v, dz=0, dy=0):
    perm = []
    for t in range(8):
        z, y = t // 4, t % 4
        perm.append((t, ((z + dz) % 2) * 4 + (y + dy) % 4))
    return lax.ppermute(v, "tp", perm)


def relative(i, major, minor):
    k = i // 2
    shift = jnp.where(k == 0, 0, jnp.where(k == 1, 3, k - 1))
    return lax.rem(major + lax.rem(i, 2), 2) * 4 + lax.rem(minor + shift, 4)


def cost(mib, flops=0):
    return pl.CostEstimate(flops=flops, bytes_accessed=int(mib * 2**20), transcendentals=0)


def concat(pieces, gates=()):
    cols = pieces[0][0].shape[-1]
    grid = 2 if cols > 512 else 1
    wide = cols // grid
    counts, specs = [], []
    for a, at in pieces:
        if at is None:
            counts.append(a.shape[0])
            specs.append(pl.BlockSpec((a.shape[0], wide), lambda i: (0, i)))
        else:
            counts.append(a.shape[1])
            specs.append(
                pl.BlockSpec((1, a.shape[1], wide), functools.partial(lambda n, i: (n, 0, i), at))
            )
    total = sum(counts)

    def kernel(*refs):
        out = refs[-1]
        row = 0
        for ref, (_, at), count in zip(refs, pieces, counts):
            out[row : row + count, :] = ref[...] if at is None else ref[0]
            row += count

    return pl.pallas_call(
        kernel,
        out_shape=jax.ShapeDtypeStruct((total, cols), bf16),
        grid=(grid,),
        in_specs=specs + [ANY] * len(gates),
        out_specs=pl.BlockSpec((total, wide), lambda i: (0, i)),
        compiler_params=LIMIT,
        cost_estimate=cost(total * cols / 2**18),
    )(*[a for a, _ in pieces], *gates)


def pack_held(ids, out_held, query_held):
    def kernel(ids_ref, out_held_ref, query_held_ref, out_ref):
        turned = out_held_ref[...].astype(f32).T.astype(bf16)
        out_ref[:, :, :512] = turned.reshape(4, 64, 512)
        out_ref[:, :, 512:] = query_held_ref[...].reshape(4, 64, 512)

    return pl.pallas_call(
        kernel,
        out_shape=jax.ShapeDtypeStruct((8, 64, 1024), bf16),
        grid_spec=pltpu.PrefetchScalarGridSpec(
            num_scalar_prefetch=1,
            grid=(2,),
            in_specs=[
                pl.BlockSpec((512, 256), lambda i, ids: (0, ids[0] * 2 + i)),
                pl.BlockSpec((256, 512), lambda i, ids: (ids[0] * 2 + i, 0)),
            ],
            out_specs=pl.BlockSpec((4, 64, 1024), lambda i, ids: (i, 0, 0)),
        ),
        compiler_params=LIMIT,
        cost_estimate=cost(2),
    )(ids, out_held, query_held)


def refreshed(master, base, held, exponent):
    power = jnp.left_shift(jnp.int32(1), exponent + 24).astype(f32) * 2.0 ** (-24)
    inverse = jnp.left_shift(jnp.int32(1), -exponent).astype(f32)
    change = master - base.astype(f32)
    code = jnp.clip(change * inverse, -code_limit, code_limit).astype(bf16)
    return (held.astype(f32) + code.astype(f32) * power).astype(bf16)


def finish_out(ids, scales, master, base, held, gates):
    def kernel(ids_ref, scales_ref, master_ref, base_ref, held_ref, *rest):
        out_ref = rest[-1]
        column = (ids_ref[0] * 8 + ids_ref[1]) // 2
        for i in range(8):
            block = relative(jnp.int32(i), ids_ref[1] // 4, lax.rem(ids_ref[1], 4))
            for q in range(4):
                lanes = pl.ds(pl.multiple_of(block * 512 + q * 128, 128), 128)
                out_ref[:, i * 512 + q * 128 : i * 512 + q * 128 + 128] = refreshed(
                    master_ref[:, lanes],
                    base_ref[:, lanes],
                    held_ref[block, :, q * 128 : q * 128 + 128],
                    scales_ref[block * 4 + q, column],
                )

    return pl.pallas_call(
        kernel,
        out_shape=jax.ShapeDtypeStruct((64, 4096), bf16),
        grid_spec=pltpu.PrefetchScalarGridSpec(
            num_scalar_prefetch=2,
            grid=(1,),
            in_specs=[
                pl.BlockSpec((64, 4096), lambda i, ids, s: (0, 0)),
                pl.BlockSpec((64, 4096), lambda i, ids, s: (0, 0)),
                pl.BlockSpec((8, 64, 512), lambda i, ids, s: (0, 0, 0)),
            ]
            + [ANY] * len(gates),
            out_specs=pl.BlockSpec((64, 4096), lambda i, ids, s: (0, 0)),
        ),
        compiler_params=LIMIT,
        cost_estimate=cost(2.5),
    )(ids, scales, master, base, held, *gates)


def finish_query(ids, scales, master, base, held, gates):
    w = 512 // CHUNKS

    def kernel(ids_ref, scales_ref, master_ref, base_ref, held_ref, *rest):
        out_ref = rest[-1]
        row = (ids_ref[0] * 8 + ids_ref[1]) // 2
        for t in range(8):
            for q in range(4):
                lanes = slice(t * 512 + q * 128, t * 512 + q * 128 + 128)
                chunk, at = q * 128 // w, t * w + q * 128 % w
                out_ref[chunk, :, at : at + 128] = refreshed(
                    master_ref[:, lanes],
                    base_ref[:, lanes],
                    held_ref[t, :, q * 128 : q * 128 + 128],
                    scales_ref[row, t * 4 + q],
                )

    return pl.pallas_call(
        kernel,
        out_shape=jax.ShapeDtypeStruct((CHUNKS, 64, 8 * w), bf16),
        grid_spec=pltpu.PrefetchScalarGridSpec(
            num_scalar_prefetch=2,
            grid=(1,),
            in_specs=[
                pl.BlockSpec((64, 4096), lambda i, ids, s: (0, 0)),
                pl.BlockSpec((64, 4096), lambda i, ids, s: (0, 0)),
                pl.BlockSpec((8, 64, 512), lambda i, ids, s: (0, 0, 1)),
            ]
            + [ANY] * len(gates),
            out_specs=pl.BlockSpec((CHUNKS, 64, 8 * w), lambda i, ids, s: (0, 0, 0)),
        ),
        compiler_params=LIMIT,
        cost_estimate=cost(2.5),
    )(ids, scales, master, base, held, *gates)


def pack_residual(ids, residual, gain, gates):
    rows = residual.shape[0]

    def kernel(ids_ref, res_own, res_other, gain_own, gain_other, *rest):
        out_ref = rest[-1]
        at = lax.broadcasted_iota(jnp.int32, (16, 128), 0)
        for t in range(8):
            lanes = slice(t * 64, t * 64 + 64)
            out_ref[t, :rows, :] = jnp.concatenate(
                [res_own[:, lanes].astype(f32), res_other[:, lanes].astype(f32)], axis=1
            ).astype(bf16)
            value = jnp.concatenate([gain_own[:, lanes], gain_other[:, lanes]], axis=1)
            high = value.astype(bf16).astype(f32)
            middle = (value - high).astype(bf16).astype(f32)
            low = value - high - middle
            out_ref[t, rows:, :] = jnp.where(
                at == 0, high, jnp.where(at == 1, middle, jnp.where(at == 2, low, 0.0))
            ).astype(bf16)

    def own(i, ids):
        return (0, lax.rem(ids[0], 2))

    def other(i, ids):
        return (0, 1 - lax.rem(ids[0], 2))

    return pl.pallas_call(
        kernel,
        out_shape=jax.ShapeDtypeStruct((8, rows + 16, 128), bf16),
        grid_spec=pltpu.PrefetchScalarGridSpec(
            num_scalar_prefetch=1,
            grid=(1,),
            in_specs=[
                pl.BlockSpec((rows, 512), own),
                pl.BlockSpec((rows, 512), other),
                pl.BlockSpec((1, 512), own),
                pl.BlockSpec((1, 512), other),
            ]
            + [ANY] * len(gates),
            out_specs=pl.BlockSpec((8, rows + 16, 128), lambda i, ids: (0, 0, 0)),
        ),
        compiler_params=LIMIT,
        cost_estimate=cost(2),
    )(ids, residual, residual, gain, gain, *gates)


def out_product(ids, att, weights, packed):
    copies = [(n, i, g) for n, (_, groups) in enumerate(weights) for i, g in enumerate(groups)]
    rows = att[0].shape[0]

    def kernel(ids_ref, *refs):
        pieces, w_refs, packed_ref = refs[:8], refs[8 : 8 + len(weights)], refs[8 + len(weights)]
        hidden_ref, squares_ref, att_buf, w_buf, res_buf, sems = refs[-6:]
        waits = []
        for k in range(8):
            lanes = pl.ds(k * 512, 512)
            pair = [pltpu.make_async_copy(pieces[k], att_buf.at[k], sems.at[k, 0])]
            for m, (n, i, g) in enumerate(copies):
                pair.append(
                    pltpu.make_async_copy(
                        w_refs[n].at[pl.ds(i * 64, 64), lanes],
                        w_buf.at[k, pl.ds(g * 64, 64)],
                        sems.at[k, m + 1],
                    )
                )
            for copy in pair:
                copy.start()
            waits.append(pair)
        last = pltpu.make_async_copy(
            packed_ref, res_buf, sems.at[8, 0]
        )
        last.start()
        total = None
        for k in range(8):
            for copy in waits[k]:
                copy.wait()
            product = lax.dot_general(
                att_buf[k], w_buf[k], NT, preferred_element_type=f32
            )
            total = product if total is None else total + product
        last.wait()
        major, minor = ids_ref[0] // 8, lax.rem(ids_ref[0] // 2, 4)
        squares = jnp.zeros((rows, 128), f32)
        for part in range(2):
            lanes = slice(part * 64, part * 64 + 64)
            for g in range(0, 8, 2):
                residual, gain = [], []
                for d in range(2):
                    group = relative(jnp.int32(g + d), major, minor)
                    residual.append(res_buf[group, :rows, :].astype(f32)[:, lanes])
                    three = res_buf[group, rows:, :].astype(f32)[:, lanes]
                    gain.append(three[0:1] + three[1:2] + three[2:3])
                at = slice(part * 512 + g * 64, part * 512 + g * 64 + 128)
                updated = total[:, at] + jnp.concatenate(residual, axis=1)
                hidden_ref[:, at] = (updated * jnp.concatenate(gain, axis=1)).astype(bf16)
                squares = squares + updated * updated
        squares_ref[...] = squares

    return pl.pallas_call(
        kernel,
        out_shape=[
            jax.ShapeDtypeStruct((rows, 1024), bf16),
            jax.ShapeDtypeStruct((rows, 128), f32),
        ],
        grid_spec=pltpu.PrefetchScalarGridSpec(
            num_scalar_prefetch=1,
            grid=(1,),
            in_specs=[ANY] * (9 + len(weights)),
            out_specs=[
                pl.BlockSpec((rows, 1024), lambda i, ids: (0, 0)),
                pl.BlockSpec((rows, 128), lambda i, ids: (0, 0)),
            ],
            scratch_shapes=[
                pltpu.VMEM((8, rows, 512), bf16),
                pltpu.VMEM((8, 1024, 512), bf16),
                pltpu.VMEM((8, rows + 16, 128), bf16),
                pltpu.SemaphoreType.DMA((9, 17)),
            ],
        ),
        compiler_params=LIMIT,
        cost_estimate=cost(14, 2 * rows * 4096 * 1024),
    )(ids, *att, *[v for v, _ in weights], packed)


def query_product(hidden, weights, extra):
    rows = hidden.shape[0]
    cols = weights[0][0].shape[1]
    w = cols // 8
    tail = 0 if extra is None else 16

    def kernel(hidden_ref, *refs):
        w_refs, out_ref = refs[: len(weights)], refs[-5]
        h_buf, w_buf, out_buf, sems = refs[-4:]
        copies = [pltpu.make_async_copy(hidden_ref, h_buf, sems.at[0])]
        for n, (w_ref, (v, row)) in enumerate(zip(w_refs, weights)):
            copies.append(
                pltpu.make_async_copy(w_ref, w_buf.at[pl.ds(row, v.shape[0])], sems.at[n + 1])
            )
        for copy in copies:
            copy.start()
        if tail:
            for t in range(8):
                out_buf[t, rows:, :] = refs[len(weights)][...]
        for copy in copies:
            copy.wait()
        sends = []
        for t in range(8):
            out_buf[t, :rows, :] = jnp.dot(
                h_buf[...], w_buf[:, t * w : t * w + w], preferred_element_type=f32
            ).astype(bf16)
            copy = pltpu.make_async_copy(
                out_buf.at[t], out_ref.at[t], sems.at[1 + len(weights) + t]
            )
            copy.start()
            sends.append(copy)
        for copy in sends:
            copy.wait()

    return pl.pallas_call(
        kernel,
        out_shape=jax.ShapeDtypeStruct((8, rows + tail, w), bf16),
        in_specs=[ANY] * (1 + len(weights))
        + ([pl.BlockSpec(memory_space=pltpu.VMEM)] if tail else []),
        out_specs=ANY,
        scratch_shapes=[
            pltpu.VMEM((rows, 1024), bf16),
            pltpu.VMEM((1024, cols), bf16),
            pltpu.VMEM((8, rows + tail, w), bf16),
            pltpu.SemaphoreType.DMA((9 + len(weights),)),
        ],
        compiler_params=LIMIT,
        cost_estimate=cost(8, 2 * rows * 1024 * cols),
    )(hidden, *[v for v, _ in weights], *([extra] if tail else []))


def split3(value):
    high = value.astype(bf16)
    middle = (value - high.astype(f32)).astype(bf16)
    low = (value - high.astype(f32) - middle.astype(f32)).astype(bf16)
    return high, middle, low


def per_device(
    out_master,
    out_base,
    out_held,
    out_scales,
    query_master,
    query_base,
    query_held,
    query_scales,
    attention,
    residual,
    norm_gain,
):
    ids = jnp.stack([lax.axis_index("rep"), lax.axis_index("tp")]).astype(jnp.int32)
    width = out_held.shape[1]
    steps = attention.shape[0]
    rows = steps * attention.shape[1]
    w = 512 // CHUNKS

    held = pack_held(ids, out_held, query_held)
    a_own = concat([(attention.reshape(rows, 512), None)], (held,))
    held = lax.all_to_all(held, "tp", 0, 0, tiled=True)

    a_par = move_tp(a_own, dz=1)
    a_l_own = move_tp(a_own, dy=1)
    a_r_own = move_tp(a_own, dy=-1)
    a_f_own = move_tp(a_l_own, dy=1)
    a_l_par = move_tp(a_par, dy=1)
    a_r_par = move_tp(a_par, dy=-1)
    a_f_par = move_tp(a_r_par, dy=-1)
    att = [a_own, a_par, a_l_own, a_l_par, a_r_own, a_r_par, a_f_own, a_f_par]

    own = finish_out(
        ids, out_scales, out_master.T, out_base.T, held, (a_par, a_l_own, a_r_own)
    )
    par = move_rep(own, dz=1)
    l_own = move_rep(own, dx=1)
    r_own = move_rep(own, dx=-1)
    blocks = finish_query(ids, query_scales, query_master, query_base, held, (own,))
    blocks_par = move_rep(blocks, dz=1)
    packed = pack_residual(
        ids, residual.reshape(rows, 1024), norm_gain.reshape(1, 1024), (own,)
    )
    packed = lax.all_to_all(packed, "tp", 0, 0, tiled=True)

    f_own = move_rep(l_own, dx=1)
    l_par = move_rep(par, dx=1)
    r_par = move_rep(par, dx=-1)
    first = concat(
        [(v, None) for v in (own, par, l_own, r_own)], (a_f_own, a_l_par, a_r_par, blocks_par)
    )

    f_par = move_rep(r_par, dx=-1)
    second = concat([(v, None) for v in (l_par, r_par, f_own)], (a_f_par,))
    weights = [
        (own, (0,)),
        (par, (1,)),
        (l_own, (2,)),
        (l_par, (3,)),
        (r_own, (4,)),
        (r_par, (5,)),
        (f_own, (6,)),
        (f_par, (7,)),
        (move_rep(first, dc=1), (8, 9, 10, 12)),
        (move_rep(second, dc=1), (11, 13, 14)),
        (move_rep(f_par, dc=1), (15,)),
    ]

    hidden, squares = out_product(ids, att, weights, packed)
    squares = jnp.stack(split3(jnp.sum(squares, axis=1))).reshape(3 * rows // w, w)
    squares = jnp.concatenate([squares, jnp.zeros((16 - 3 * rows // w, w), bf16)], axis=0)

    sums = []
    gates = (l_par, r_par, f_own)
    before = hidden
    for j in range(CHUNKS):
        own = concat([(blocks, j), (blocks_par, j)], gates)
        left = move_rep(own, dx=1)
        right = move_rep(own, dx=-1)
        gates = (left, right)
        far_a = move_rep(left[:64], dx=1)
        far_b = move_rep(right[64:], dx=-1)
        near = concat([(v, None) for v in (own, left, right)], (before,))
        far = concat([(v, None) for v in (far_a, far_b)], (before,))
        weights = [
            (own, 0),
            (left, 128),
            (right, 256),
            (far_a, 384),
            (far_b, 448),
            (move_rep(near, dc=1), 512),
            (move_rep(far, dc=1), 896),
        ]
        partial = query_product(hidden, weights, squares if j == 0 else None)
        before = partial
        sums.append(lax.all_to_all(partial, "tp", 0, 0, tiled=True))
    squares = sums[0][:, rows:].astype(f32).reshape(8, -1)[:, : 3 * rows].reshape(8, 3, rows)
    inverse = lax.rsqrt(jnp.sum(squares, axis=(0, 1)) / width + 1e-06)[:, None]
    outs = [
        (jnp.sum(part[:, :rows].astype(f32), axis=0) * inverse).astype(bf16) for part in sums
    ]
    return jnp.concatenate(outs, axis=1).reshape(steps, rows // steps, 512)


def solution(mesh):
    placed = (
        P(None, ("rep", "tp")),
        P(None, ("rep", "tp")),
        P("tp", None),
        P(),
        P(("rep", "tp"), None),
        P(("rep", "tp"), None),
        P(None, "tp"),
        P(),
        P(None, "rep", "tp"),
        P(None, "rep", "tp"),
        P("tp"),
    )
    return jax.shard_map(
        per_device, mesh=mesh, in_specs=placed, out_specs=P(None, "rep", "tp"), check_vma=False
    )
```

profile of v0, /device:TPU:1, one launch (start us, length us, event | category | flops | bytes accessed | tf_op | source)
XLA Modules:
  0.0 222.2 jit_solution(2392337577378662832)
XLA Ops:
  0.1 2.7 %shard_map.109.refs_1_ = bf16[8,64,1024]{2,1,0:T(8,128)(2,1)} custom-call(s32[2]{0:T(128)S(1)} %pad_add_fusion.ids_ref, bf16[512,8192]{1,0:T(8,128)(2,1)} %out_held_ref.1, bf16[8192,512]{1,0:T(8,128)(2,1)} %query_held_ref.1), custom_call_target="tpu_custom_call" | custom-call | bytes 2097152 | tf_op jit(solution)/shard_map/pallas_call | solution.py:86
  3.7 2.5 %collective-permute-start = (bf16[512,512]{1,0:T(8,128)(2,1)}, bf16[512,512]{1,0:T(8,128)(2,1)}, u32[]{:S(2)}, u32[]{:S(2)}) collective-permute-start(bf16[512,512]{1,0:T(8,128)(2,1)} %shard_map.110.refs_0_), channel_id=1, source_target_pairs={{0,4},{1,5},{2,6},{3,7},{4,0},{5,1},{6,2},{7,3},{8,12},{9,13},{10,... | collective-permute-start | bytes 1572872 | tf_op jit(solution)/shard_map/ppermute | solution.py:33
  6.1 4.2 %all-to-all-start = ((bf16[8,64,1024]{2,1,0:T(8,128)(2,1)}), bf16[8,64,1024]{2,1,0:T(8,128)(2,1)S(1)}, u32[]{:S(2)}, u32[]{:S(2)}) async-start(bf16[8,64,1024]{2,1,0:T(8,128)(2,1)} %shard_map.109.refs_1_), calls=%async_computation | async-start | bytes 2097152 | tf_op jit(solution)/shard_map/all_to_all | solution.py:383
  10.3 1.5 collective-permute-start.1
  11.8 1.2 collective-permute-start.3
  13.0 12.2 %collective-permute-done.rest_0_.refs_1_ = bf16[512,512]{1,0:T(8,128)(2,1)} collective-permute-done((bf16[512,512]{1,0:T(8,128)(2,1)}, bf16[512,512]{1,0:T(8,128)(2,1)}, u32[]{:S(2)}, u32[]{:S(2)}) %collective-permute-start) | collective-permute-done | bytes 524320 | tf_op jit(solution)/shard_map/ppermute | solution.py:33
  25.8 3.3 %collective-permute-start.4 = (bf16[512,512]{1,0:T(8,128)(2,1)}, bf16[512,512]{1,0:T(8,128)(2,1)}, u32[]{:S(2)}, u32[]{:S(2)}) collective-permute-start(bf16[512,512]{1,0:T(8,128)(2,1)} %collective-permute-done.rest_0_.refs_1_), channel_id=1, source_target_pairs={{0,3},{1,0},{2,1},{3,2},{4,7},{5,4},{6,5},{7,6},{8,11},{9,8},{10,9... | collective-permute-start | bytes 1572872 | tf_op jit(solution)/shard_map/ppermute | solution.py:33
  29.2 7.3 %collective-permute-done.1.rest_1_.refs_2_ = bf16[512,512]{1,0:T(8,128)(2,1)} collective-permute-done((bf16[512,512]{1,0:T(8,128)(2,1)}, bf16[512,512]{1,0:T(8,128)(2,1)}, u32[]{:S(2)}, u32[]{:S(2)}) %collective-permute-start.1) | collective-permute-done | bytes 524320 | tf_op jit(solution)/shard_map/ppermute | solution.py:33
  39.6 3.4 %collective-permute-start.7 = (bf16[64,4096]{1,0:T(8,128)(2,1)S(1)}, bf16[64,4096]{1,0:T(8,128)(2,1)S(1)}, u32[]{:S(2)}, u32[]{:S(2)}) collective-permute-start(bf16[64,4096]{1,0:T(8,128)(2,1)S(1)} %shard_map.111.rest_0_.refs_0_.refs_8_), channel_id=1, source_target_pairs={{0,64},{8,72},{16,80},{24,88},{32,96},{40,104},{48,112},{56,120},{... | collective-permute-start | bytes 1572872 | tf_op jit(solution)/shard_map/ppermute | solution.py:25
  43.0 1.2 collective-permute-start.8
  44.2 1.4 shard_map.112.refs_0_
  45.7 2.1 collective-permute-done.2.refs_5_.refs_3_
  47.8 2.5 %collective-permute-start.10 = (bf16[64,4096]{1,0:T(8,128)(2,1)S(1)}, bf16[64,4096]{1,0:T(8,128)(2,1)S(1)}, u32[]{:S(2)}, u32[]{:S(2)}) collective-permute-start(bf16[64,4096]{1,0:T(8,128)(2,1)S(1)} %shard_map.111.rest_0_.refs_0_.refs_8_), channel_id=1, source_target_pairs={{0,48},{8,56},{16,0},{24,8},{32,16},{40,24},{48,32},{56,40},{64,11... | collective-permute-start | bytes 1572872 | tf_op jit(solution)/shard_map/ppermute | solution.py:25
  50.3 3.3 %collective-permute-start.14 = (bf16[2,64,2048]{2,1,0:T(8,128)(2,1)S(1)}, bf16[2,64,2048]{2,1,0:T(8,128)(2,1)S(1)}, u32[]{:S(2)}, u32[]{:S(2)}) collective-permute-start(bf16[2,64,2048]{2,1,0:T(8,128)(2,1)S(1)} %shard_map.112.refs_0_), channel_id=1, source_target_pairs={{0,64},{8,72},{16,80},{24,88},{32,96},{40,104},{48,112},{56,120},{... | collective-permute-start | bytes 1572872 | tf_op jit(solution)/shard_map/ppermute | solution.py:25
  53.6 5.4 %collective-permute-done.5.refs_4_.refs_6_ = bf16[512,512]{1,0:T(8,128)(2,1)} collective-permute-done((bf16[512,512]{1,0:T(8,128)(2,1)}, bf16[512,512]{1,0:T(8,128)(2,1)}, u32[]{:S(2)}, u32[]{:S(2)}) %collective-permute-start.5) | collective-permute-done | bytes 524320 | tf_op jit(solution)/shard_map/ppermute | solution.py:33
  59.1 1.3 collective-permute-start.9
  60.3 1.5 collective-permute-start.11
  61.8 3.7 %collective-permute-done.14.refs_7_.refs_1_ = bf16[2,64,2048]{2,1,0:T(8,128)(2,1)S(1)} collective-permute-done((bf16[2,64,2048]{2,1,0:T(8,128)(2,1)S(1)}, bf16[2,64,2048]{2,1,0:T(8,128)(2,1)S(1)}, u32[]{:S(2)}, u32[]{:S(2)}) %collective-permute-start.14) | collective-permute-done | bytes 524320 | tf_op jit(solution)/shard_map/ppermute | solution.py:25
  65.5 1.6 shard_map.113
  68.0 1.6 collective-permute-start.15
  69.5 2.3 %collective-permute-done.6.refs_3_.refs_7_ = bf16[512,512]{1,0:T(8,128)(2,1)S(1)} collective-permute-done((bf16[512,512]{1,0:T(8,128)(2,1)}, bf16[512,512]{1,0:T(8,128)(2,1)S(1)}, u32[]{:S(2)}, u32[]{:S(2)}) %collective-permute-start.6) | collective-permute-done | bytes 524320 | tf_op jit(solution)/shard_map/ppermute | solution.py:33
  72.1 11.2 %collective-permute-done.12.refs_2_.refs_14_.refs_4_ = bf16[64,4096]{1,0:T(8,128)(2,1)S(1)} collective-permute-done((bf16[64,4096]{1,0:T(8,128)(2,1)S(1)}, bf16[64,4096]{1,0:T(8,128)(2,1)S(1)}, u32[]{:S(2)}, u32[]{:S(2)}) %collective-permute-start.12) | collective-permute-done | bytes 524320 | tf_op jit(solution)/shard_map/ppermute | solution.py:25
  83.3 1.3 shard_map.114
  84.7 2.6 %collective-permute-start.16 = (bf16[192,4096]{1,0:T(8,128)(2,1)}, bf16[192,4096]{1,0:T(8,128)(2,1)}, u32[]{:S(2)}, u32[]{:S(2)}) collective-permute-start(bf16[192,4096]{1,0:T(8,128)(2,1)} %shard_map.114), channel_id=1, source_target_pairs={{0,8},{8,0},{16,24},{24,16},{32,40},{40,32},{48,56},{56,48},{64,72... | collective-permute-start | bytes 4718600 | tf_op jit(solution)/shard_map/ppermute | solution.py:25
  87.3 1.3 collective-permute-start.13
  88.5 2.0 shard_map.115
  90.5 4.3 %all-to-all-start.1 = ((bf16[8,528,128]{2,1,0:T(8,128)(2,1)}), bf16[8,528,128]{2,1,0:T(8,128)(2,1)}, u32[]{:S(2)}, u32[]{:S(2)}) async-start(bf16[8,528,128]{2,1,0:T(8,128)(2,1)} %shard_map.115), calls=%async_computation.1 | async-start | bytes 2162688 | tf_op jit(solution)/shard_map/all_to_all | solution.py:405
  94.8 6.1 %collective-permute-done.13.refs_15_ = bf16[64,4096]{1,0:T(8,128)(2,1)} collective-permute-done((bf16[64,4096]{1,0:T(8,128)(2,1)S(1)}, bf16[64,4096]{1,0:T(8,128)(2,1)}, u32[]{:S(2)}, u32[]{:S(2)}) %collective-permute-start.13) | collective-permute-done | bytes 524320 | tf_op jit(solution)/shard_map/ppermute | solution.py:25
  102.6 2.7 %collective-permute-start.19 = (bf16[128,2048]{1,0:T(8,128)(2,1)}, bf16[128,2048]{1,0:T(8,128)(2,1)S(1)}, u32[]{:S(2)}, u32[]{:S(2)}) collective-permute-start(bf16[128,2048]{1,0:T(8,128)(2,1)} %shard_map.117.refs_0_), channel_id=1, source_target_pairs={{0,48},{8,56},{16,0},{24,8},{32,16},{40,24},{48,32},{56,40},{64,11... | collective-permute-start | bytes 1572872 | tf_op jit(solution)/shard_map/ppermute | solution.py:25
  105.3 5.8 %all-to-all-done.1.refs_19_ = bf16[8,528,128]{2,1,0:T(8,128)(2,1)} async-done(((bf16[8,528,128]{2,1,0:T(8,128)(2,1)}), bf16[8,528,128]{2,1,0:T(8,128)(2,1)}, u32[]{:S(2)}, u32[]{:S(2)}) %all-to-all-start.1) | async-done | bytes 1081376 | tf_op jit(solution)/shard_map/all_to_all | solution.py:405
  115.3 10.6 %shard_map.116 = (bf16[512,1024]{1,0:T(8,128)(2,1)}, f32[512,128]{1,0:T(8,128)S(1)}) custom-call(s32[2]{0:T(128)S(1)} %pad_add_fusion.ids_ref, bf16[512,512]{1,0:T(8,128)(2,1)} %shard_map.110.refs_0_, bf16[512,512]{1,0:T(8,128)(2,1)} %collective-permute-done.rest_0_.refs_1_, bf16[512,512]{1,0:T(8,128)(2,1)} %collective-permute-done.1.rest_1_.refs_2_, ...), custom_call_target="tpu_custom_call" | custom-call | flops 4294967296 | bytes 14680064 | tf_op jit(solution)/shard_map/pallas_call | solution.py:278
  126.7 1.2 copy-done.1
  129.0 2.3 %shard_map.118 = bf16[384,2048]{1,0:T(8,128)(2,1)} custom-call(bf16[128,2048]{1,0:T(8,128)(2,1)} %shard_map.117.refs_0_, bf16[128,2048]{1,0:T(8,128)(2,1)S(1)} %collective-permute-done.18.refs_1_.refs_2_, bf16[128,2048]{1,0:T(8,128)(2,1)S(1)} %copy-done.5, bf16[512,1024]{1,0:T(8,128)(2,1)S(1)} %copy-done.1), custom_call_target="tpu_custom_call" | custom-call | bytes 3145728 | tf_op jit(solution)/shard_map/pallas_call | solution.py:69
  132.3 2.6 %collective-permute-start.21 = (bf16[64,2048]{1,0:T(8,128)(2,1)S(1)}, bf16[64,2048]{1,0:T(8,128)(2,1)S(1)}, u32[]{:S(2)}, u32[]{:S(2)}) collective-permute-start(bf16[64,2048]{1,0:T(8,128)(2,1)S(1)} %slice.33), channel_id=1, source_target_pairs={{0,48},{8,56},{16,0},{24,8},{32,16},{40,24},{48,32},{56,40},{64,11... | collective-permute-start | bytes 786440 | tf_op jit(solution)/shard_map/ppermute | solution.py:25
  134.9 6.4 %collective-permute-done.20.refs_0_.refs_3_ = bf16[64,2048]{1,0:T(8,128)(2,1)S(1)} collective-permute-done((bf16[64,2048]{1,0:T(8,128)(2,1)S(1)}, bf16[64,2048]{1,0:T(8,128)(2,1)S(1)}, u32[]{:S(2)}, u32[]{:S(2)}) %collective-permute-start.20) | collective-permute-done | bytes 262176 | tf_op jit(solution)/shard_map/ppermute | solution.py:25
  143.9 2.8 %collective-permute-start.25 = (bf16[128,2048]{1,0:T(8,128)(2,1)}, bf16[128,2048]{1,0:T(8,128)(2,1)}, u32[]{:S(2)}, u32[]{:S(2)}) collective-permute-start(bf16[128,2048]{1,0:T(8,128)(2,1)} %shard_map.121.refs_0_), channel_id=1, source_target_pairs={{0,48},{8,56},{16,0},{24,8},{32,16},{40,24},{48,32},{56,40},{64,11... | collective-permute-start | bytes 1572872 | tf_op jit(solution)/shard_map/ppermute | solution.py:25
  148.8 5.1 %shard_map.120.refs_3_.refs_2_ = bf16[8,528,256]{2,1,0:T(8,128)(2,1)} custom-call(bf16[512,1024]{1,0:T(8,128)(2,1)S(1)} %copy-done.2, bf16[128,2048]{1,0:T(8,128)(2,1)} %shard_map.117.refs_0_, bf16[128,2048]{1,0:T(8,128)(2,1)S(1)} %collective-permute-done.18.refs_1_.refs_2_, bf16[128,2048]{1,0:T(8,128)(2,1)S(1)} %copy-done.5, ...), custom_call_target="tpu_custom_call" | custom-call | flops 2147483648 | bytes 8388608 | tf_op jit(solution)/shard_map/pallas_call | solution.py:338
  153.9 4.5 %all-to-all-start.2 = ((bf16[8,528,256]{2,1,0:T(8,128)(2,1)}), bf16[8,528,256]{2,1,0:T(8,128)(2,1)}, u32[]{:S(2)}, u32[]{:S(2)}) async-start(bf16[8,528,256]{2,1,0:T(8,128)(2,1)} %shard_map.120.refs_3_.refs_2_), calls=%async_computation.2 | async-start | bytes 4325376 | tf_op jit(solution)/shard_map/all_to_all | solution.py:457
  159.0 1.5 shard_map.122
  164.2 1.9 collective-permute-start.27
  166.2 5.6 %collective-permute-done.26.refs_0_.refs_3_ = bf16[64,2048]{1,0:T(8,128)(2,1)S(1)} collective-permute-done((bf16[64,2048]{1,0:T(8,128)(2,1)S(1)}, bf16[64,2048]{1,0:T(8,128)(2,1)S(1)}, u32[]{:S(2)}, u32[]{:S(2)}) %collective-permute-start.26) | collective-permute-done | bytes 262176 | tf_op jit(solution)/shard_map/ppermute | solution.py:25
  172.2 1.3 collective-permute-start.29
  173.5 1.5 collective-permute-done.29.refs_6_
  175.0 4.8 %shard_map.124 = bf16[8,512,256]{2,1,0:T(8,128)(2,1)} custom-call(bf16[512,1024]{1,0:T(8,128)(2,1)S(1)} %copy-done.2, bf16[128,2048]{1,0:T(8,128)(2,1)} %shard_map.121.refs_0_, bf16[128,2048]{1,0:T(8,128)(2,1)} %collective-permute-done.24.refs_1_, bf16[128,2048]{1,0:T(8,128)(2,1)} %collective-permute-done.25.refs_2_, ...), custom_call_target="tpu_custom_call" | custom-call | flops 2147483648 | bytes 8388608 | tf_op jit(solution)/shard_map/pallas_call | solution.py:338
  179.8 6.5 %all-to-all-done.2 = bf16[8,528,256]{2,1,0:T(8,128)(2,1)} async-done(((bf16[8,528,256]{2,1,0:T(8,128)(2,1)}), bf16[8,528,256]{2,1,0:T(8,128)(2,1)}, u32[]{:S(2)}, u32[]{:S(2)}) %all-to-all-start.2) | async-done | bytes 2162720 | tf_op jit(solution)/shard_map/all_to_all | solution.py:457
  186.3 7.6 %all-to-all-start.3 = ((bf16[8,512,256]{2,1,0:T(8,128)(2,1)}), bf16[8,512,256]{2,1,0:T(8,128)(2,1)S(1)}, u32[]{:S(2)}, u32[]{:S(2)}) async-start(bf16[8,512,256]{2,1,0:T(8,128)(2,1)} %shard_map.124), calls=%async_computation.3 | async-start | bytes 4194304 | tf_op jit(solution)/shard_map/all_to_all | solution.py:457
  194.8 1.9 convert_reduce_fusion.1
  196.7 24.2 %all-to-all-done.3 = bf16[8,512,256]{2,1,0:T(8,128)(2,1)S(1)} async-done(((bf16[8,512,256]{2,1,0:T(8,128)(2,1)}), bf16[8,512,256]{2,1,0:T(8,128)(2,1)S(1)}, u32[]{:S(2)}, u32[]{:S(2)}) %all-to-all-start.3) | async-done | bytes 2097184 | tf_op jit(solution)/shard_map/all_to_all | solution.py:457
  (120 shorter events, 26.0 us)
Async XLA Ops:
  2.8 26.3 %copy-start.30 = (s32[64,32]{0,1:T(8,128)S(1)}, s32[64,32]{0,1:T(8,128)}, u32[]{:S(2)}) copy-start(s32[64,32]{0,1:T(8,128)} %param.18) | copy-start | bytes 24580
  2.8 34.6 %copy-start.9 = (f32[4096,64]{0,1:T(8,128)S(1)}, f32[4096,64]{0,1:T(8,128)}, u32[]{:S(2)}) copy-start(f32[4096,64]{0,1:T(8,128)} %param.11) | copy-start | bytes 3145732
  2.8 34.6 %copy-start.11 = (bf16[4096,64]{0,1:T(8,128)(2,1)S(1)}, bf16[4096,64]{0,1:T(8,128)(2,1)}, u32[]{:S(2)}) copy-start(bf16[4096,64]{0,1:T(8,128)(2,1)} %param.12) | copy-start | bytes 1572868
  2.8 34.5 %copy-start.28 = (s32[32,64]{1,0:T(8,128)S(1)}, s32[32,64]{1,0:T(8,128)}, u32[]{:S(2)}) copy-start(s32[32,64]{1,0:T(8,128)} %scales_ref.2) | copy-start | bytes 24580
  3.7 21.5 %collective-permute-start = (bf16[512,512]{1,0:T(8,128)(2,1)}, bf16[512,512]{1,0:T(8,128)(2,1)}, u32[]{:S(2)}, u32[]{:S(2)}) collective-permute-start(bf16[512,512]{1,0:T(8,128)(2,1)} %shard_map.110.refs_0_), channel_id=1, source_target_pairs={{0,4},{1,5},{2,6},{3,7},{4,0},{5,1},{6,2},{7,3},{8,12},{9,13},{10,... | collective-permute-start | bytes 1572872 | tf_op jit(solution)/shard_map/ppermute | solution.py:33
  6.1 31.2 %all-to-all-start = ((bf16[8,64,1024]{2,1,0:T(8,128)(2,1)}), bf16[8,64,1024]{2,1,0:T(8,128)(2,1)S(1)}, u32[]{:S(2)}, u32[]{:S(2)}) async-start(bf16[8,64,1024]{2,1,0:T(8,128)(2,1)} %shard_map.109.refs_1_), calls=%async_computation | async-start | bytes 2097152 | tf_op jit(solution)/shard_map/all_to_all | solution.py:383
  10.3 26.2 %collective-permute-start.1 = (bf16[512,512]{1,0:T(8,128)(2,1)}, bf16[512,512]{1,0:T(8,128)(2,1)}, u32[]{:S(2)}, u32[]{:S(2)}) collective-permute-start(bf16[512,512]{1,0:T(8,128)(2,1)} %shard_map.110.refs_0_), channel_id=1, source_target_pairs={{0,1},{1,2},{2,3},{3,0},{4,5},{5,6},{6,7},{7,4},{8,9},{9,10},{10,1... | collective-permute-start | bytes 1572872 | tf_op jit(solution)/shard_map/ppermute | solution.py:33
  11.8 24.8 %collective-permute-start.3 = (bf16[512,512]{1,0:T(8,128)(2,1)}, bf16[512,512]{1,0:T(8,128)(2,1)S(1)}, u32[]{:S(2)}, u32[]{:S(2)}) collective-permute-start(bf16[512,512]{1,0:T(8,128)(2,1)} %shard_map.110.refs_0_), channel_id=1, source_target_pairs={{0,3},{1,0},{2,1},{3,2},{4,7},{5,4},{6,5},{7,6},{8,11},{9,8},{10,9... | collective-permute-start | bytes 1572872 | tf_op jit(solution)/shard_map/ppermute | solution.py:33
  25.2 22.6 %collective-permute-start.2 = (bf16[512,512]{1,0:T(8,128)(2,1)}, bf16[512,512]{1,0:T(8,128)(2,1)}, u32[]{:S(2)}, u32[]{:S(2)}) collective-permute-start(bf16[512,512]{1,0:T(8,128)(2,1)} %collective-permute-done.rest_0_.refs_1_), channel_id=1, source_target_pairs={{0,1},{1,2},{2,3},{3,0},{4,5},{5,6},{6,7},{7,4},{8,9},{9,10},{10,1... | collective-permute-start | bytes 1572872 | tf_op jit(solution)/shard_map/ppermute | solution.py:33
  25.8 24.5 %collective-permute-start.4 = (bf16[512,512]{1,0:T(8,128)(2,1)}, bf16[512,512]{1,0:T(8,128)(2,1)}, u32[]{:S(2)}, u32[]{:S(2)}) collective-permute-start(bf16[512,512]{1,0:T(8,128)(2,1)} %collective-permute-done.rest_0_.refs_1_), channel_id=1, source_target_pairs={{0,3},{1,0},{2,1},{3,2},{4,7},{5,4},{6,5},{7,6},{8,11},{9,8},{10,9... | collective-permute-start | bytes 1572872 | tf_op jit(solution)/shard_map/ppermute | solution.py:33
  36.6 22.5 %collective-permute-start.5 = (bf16[512,512]{1,0:T(8,128)(2,1)}, bf16[512,512]{1,0:T(8,128)(2,1)}, u32[]{:S(2)}, u32[]{:S(2)}) collective-permute-start(bf16[512,512]{1,0:T(8,128)(2,1)} %collective-permute-done.1.rest_1_.refs_2_), channel_id=1, source_target_pairs={{0,1},{1,2},{2,3},{3,0},{4,5},{5,6},{6,7},{7,4},{8,9},{9,10},{10,1... | collective-permute-start | bytes 1572872 | tf_op jit(solution)/shard_map/ppermute | solution.py:33
  38.4 5.8 %copy-start.23 = (bf16[64,4096]{1,0:T(8,128)(2,1)S(1)}, bf16[64,4096]{1,0:T(8,128)(2,1)}, u32[]{:S(2)}) copy-start(bf16[64,4096]{1,0:T(8,128)(2,1)} %base_ref.1) | copy-start | bytes 1572868
  39.6 19.4 %collective-permute-start.7 = (bf16[64,4096]{1,0:T(8,128)(2,1)S(1)}, bf16[64,4096]{1,0:T(8,128)(2,1)S(1)}, u32[]{:S(2)}, u32[]{:S(2)}) collective-permute-start(bf16[64,4096]{1,0:T(8,128)(2,1)S(1)} %shard_map.111.rest_0_.refs_0_.refs_8_), channel_id=1, source_target_pairs={{0,64},{8,72},{16,80},{24,88},{32,96},{40,104},{48,112},{56,120},{... | collective-permute-start | bytes 1572872 | tf_op jit(solution)/shard_map/ppermute | solution.py:25
  43.0 17.3 %collective-permute-start.8 = (bf16[64,4096]{1,0:T(8,128)(2,1)S(1)}, bf16[64,4096]{1,0:T(8,128)(2,1)S(1)}, u32[]{:S(2)}, u32[]{:S(2)}) collective-permute-start(bf16[64,4096]{1,0:T(8,128)(2,1)S(1)} %shard_map.111.rest_0_.refs_0_.refs_8_), channel_id=1, source_target_pairs={{0,16},{8,24},{16,32},{24,40},{32,48},{40,56},{48,0},{56,8},{64,80... | collective-permute-start | bytes 1572872 | tf_op jit(solution)/shard_map/ppermute | solution.py:25
  47.8 14.0 %collective-permute-start.10 = (bf16[64,4096]{1,0:T(8,128)(2,1)S(1)}, bf16[64,4096]{1,0:T(8,128)(2,1)S(1)}, u32[]{:S(2)}, u32[]{:S(2)}) collective-permute-start(bf16[64,4096]{1,0:T(8,128)(2,1)S(1)} %shard_map.111.rest_0_.refs_0_.refs_8_), channel_id=1, source_target_pairs={{0,48},{8,56},{16,0},{24,8},{32,16},{40,24},{48,32},{56,40},{64,11... | collective-permute-start | bytes 1572872 | tf_op jit(solution)/shard_map/ppermute | solution.py:25
  50.3 15.2 %collective-permute-start.14 = (bf16[2,64,2048]{2,1,0:T(8,128)(2,1)S(1)}, bf16[2,64,2048]{2,1,0:T(8,128)(2,1)S(1)}, u32[]{:S(2)}, u32[]{:S(2)}) collective-permute-start(bf16[2,64,2048]{2,1,0:T(8,128)(2,1)S(1)} %shard_map.112.refs_0_), channel_id=1, source_target_pairs={{0,64},{8,72},{16,80},{24,88},{32,96},{40,104},{48,112},{56,120},{... | collective-permute-start | bytes 1572872 | tf_op jit(solution)/shard_map/ppermute | solution.py:25
  59.1 12.8 %collective-permute-start.6 = (bf16[512,512]{1,0:T(8,128)(2,1)}, bf16[512,512]{1,0:T(8,128)(2,1)S(1)}, u32[]{:S(2)}, u32[]{:S(2)}) collective-permute-start(bf16[512,512]{1,0:T(8,128)(2,1)} %collective-permute-done.4.refs_6_.refs_5_), channel_id=1, source_target_pairs={{0,3},{1,0},{2,1},{3,2},{4,7},{5,4},{6,5},{7,6},{8,11},{9,8},{10,9... | collective-permute-start | bytes 1572872 | tf_op jit(solution)/shard_map/ppermute | solution.py:33
  59.1 8.1 %copy-start.15 = (bf16[64,4096]{1,0:T(8,128)(2,1)}, bf16[64,4096]{1,0:T(8,128)(2,1)S(1)}, u32[]{:S(2)}) copy-start(bf16[64,4096]{1,0:T(8,128)(2,1)S(1)} %collective-permute-done.7.refs_1_.refs_9_) | copy-start | bytes 1572868
  59.1 13.0 %collective-permute-start.9 = (bf16[64,4096]{1,0:T(8,128)(2,1)S(1)}, bf16[64,4096]{1,0:T(8,128)(2,1)S(1)}, u32[]{:S(2)}, u32[]{:S(2)}) collective-permute-start(bf16[64,4096]{1,0:T(8,128)(2,1)S(1)} %collective-permute-done.7.refs_1_.refs_9_), channel_id=1, source_target_pairs={{0,16},{8,24},{16,32},{24,40},{32,48},{40,56},{48,0},{56,8},{64,80... | collective-permute-start | bytes 1572872 | tf_op jit(solution)/shard_map/ppermute | solution.py:25
  60.3 6.8 %copy-start.17 = (bf16[64,4096]{1,0:T(8,128)(2,1)}, bf16[64,4096]{1,0:T(8,128)(2,1)S(1)}, u32[]{:S(2)}) copy-start(bf16[64,4096]{1,0:T(8,128)(2,1)S(1)} %collective-permute-done.8.refs_2_.refs_10_) | copy-start | bytes 1572868
  60.3 11.7 %collective-permute-start.11 = (bf16[64,4096]{1,0:T(8,128)(2,1)S(1)}, bf16[64,4096]{1,0:T(8,128)(2,1)S(1)}, u32[]{:S(2)}, u32[]{:S(2)}) collective-permute-start(bf16[64,4096]{1,0:T(8,128)(2,1)S(1)} %collective-permute-done.7.refs_1_.refs_9_), channel_id=1, source_target_pairs={{0,48},{8,56},{16,0},{24,8},{32,16},{40,24},{48,32},{56,40},{64,11... | collective-permute-start | bytes 1572872 | tf_op jit(solution)/shard_map/ppermute | solution.py:25
  61.8 21.5 %collective-permute-start.12 = (bf16[64,4096]{1,0:T(8,128)(2,1)S(1)}, bf16[64,4096]{1,0:T(8,128)(2,1)S(1)}, u32[]{:S(2)}, u32[]{:S(2)}) collective-permute-start(bf16[64,4096]{1,0:T(8,128)(2,1)S(1)} %collective-permute-done.8.refs_2_.refs_10_), channel_id=1, source_target_pairs={{0,16},{8,24},{16,32},{24,40},{32,48},{40,56},{48,0},{56,8},{64,80... | collective-permute-start | bytes 1572872 | tf_op jit(solution)/shard_map/ppermute | solution.py:25
  67.9 20.6 %copy-start.3 = (bf16[4,128,1024]{2,1,0:T(8,128)(2,1)S(1)}, bf16[4,128,1024]{2,1,0:T(8,128)(2,1)}, u32[]{:S(2)}) copy-start(bf16[4,128,1024]{2,1,0:T(8,128)(2,1)} %param.20) | copy-start | bytes 3145732
  67.9 20.6 %copy-start.29 = (f32[1024]{0:T(1024)S(1)}, f32[1024]{0:T(1024)}, u32[]{:S(2)}) copy-start(f32[1024]{0:T(1024)} %param.21) | copy-start | bytes 12292
  68.0 43.1 %collective-permute-start.15 = (bf16[256,4096]{1,0:T(8,128)(2,1)}, bf16[256,4096]{1,0:T(8,128)(2,1)}, u32[]{:S(2)}, u32[]{:S(2)}) collective-permute-start(bf16[256,4096]{1,0:T(8,128)(2,1)} %shard_map.113), channel_id=1, source_target_pairs={{0,8},{8,0},{16,24},{24,16},{32,40},{40,32},{48,56},{56,48},{64,72... | collective-permute-start | bytes 6291464 | tf_op jit(solution)/shard_map/ppermute | solution.py:25
  71.8 12.8 %copy-start.20 = (bf16[512,512]{1,0:T(8,128)(2,1)}, bf16[512,512]{1,0:T(8,128)(2,1)S(1)}, u32[]{:S(2)}) copy-start(bf16[512,512]{1,0:T(8,128)(2,1)S(1)} %collective-permute-done.6.refs_3_.refs_7_) | copy-start | bytes 1572868
  72.1 29.6 %copy-start.6 = (bf16[64,4096]{1,0:T(8,128)(2,1)}, bf16[64,4096]{1,0:T(8,128)(2,1)S(1)}, u32[]{:S(2)}) copy-start(bf16[64,4096]{1,0:T(8,128)(2,1)S(1)} %collective-permute-done.9.refs_0_.refs_11_.refs_2_) | copy-start | bytes 1572868
  72.1 29.6 %copy-start.7 = (bf16[64,4096]{1,0:T(8,128)(2,1)}, bf16[64,4096]{1,0:T(8,128)(2,1)S(1)}, u32[]{:S(2)}) copy-start(bf16[64,4096]{1,0:T(8,128)(2,1)S(1)} %collective-permute-done.11.refs_1_.refs_13_.refs_3_) | copy-start | bytes 1572868
  83.3 18.4 %copy-start.8 = (bf16[64,4096]{1,0:T(8,128)(2,1)}, bf16[64,4096]{1,0:T(8,128)(2,1)S(1)}, u32[]{:S(2)}) copy-start(bf16[64,4096]{1,0:T(8,128)(2,1)S(1)} %collective-permute-done.12.refs_2_.refs_14_.refs_4_) | copy-start | bytes 1572868
  84.7 26.4 %collective-permute-start.16 = (bf16[192,4096]{1,0:T(8,128)(2,1)}, bf16[192,4096]{1,0:T(8,128)(2,1)}, u32[]{:S(2)}, u32[]{:S(2)}) collective-permute-start(bf16[192,4096]{1,0:T(8,128)(2,1)} %shard_map.114), channel_id=1, source_target_pairs={{0,8},{8,0},{16,24},{24,16},{32,40},{40,32},{48,56},{56,48},{64,72... | collective-permute-start | bytes 4718600 | tf_op jit(solution)/shard_map/ppermute | solution.py:25
  87.3 13.7 %collective-permute-start.13 = (bf16[64,4096]{1,0:T(8,128)(2,1)S(1)}, bf16[64,4096]{1,0:T(8,128)(2,1)}, u32[]{:S(2)}, u32[]{:S(2)}) collective-permute-start(bf16[64,4096]{1,0:T(8,128)(2,1)S(1)} %collective-permute-done.11.refs_1_.refs_13_.refs_3_), channel_id=1, source_target_pairs={{0,48},{8,56},{16,0},{24,8},{32,16},{40,24},{48,32},{56,40},{64,11... | collective-permute-start | bytes 1572872 | tf_op jit(solution)/shard_map/ppermute | solution.py:25
  90.5 20.5 %all-to-all-start.1 = ((bf16[8,528,128]{2,1,0:T(8,128)(2,1)}), bf16[8,528,128]{2,1,0:T(8,128)(2,1)}, u32[]{:S(2)}, u32[]{:S(2)}) async-start(bf16[8,528,128]{2,1,0:T(8,128)(2,1)} %shard_map.115), calls=%async_computation.1 | async-start | bytes 2162688 | tf_op jit(solution)/shard_map/all_to_all | solution.py:405
  100.9 10.2 %collective-permute-start.17 = (bf16[64,4096]{1,0:T(8,128)(2,1)}, bf16[64,4096]{1,0:T(8,128)(2,1)}, u32[]{:S(2)}, u32[]{:S(2)}) collective-permute-start(bf16[64,4096]{1,0:T(8,128)(2,1)} %collective-permute-done.13.refs_15_), channel_id=1, source_target_pairs={{0,8},{8,0},{16,24},{24,16},{32,40},{40,32},{48,56},{56,48},{64,72... | collective-permute-start | bytes 1572872 | tf_op jit(solution)/shard_map/ppermute | solution.py:25
  102.6 23.3 %collective-permute-start.18 = (bf16[128,2048]{1,0:T(8,128)(2,1)}, bf16[128,2048]{1,0:T(8,128)(2,1)S(1)}, u32[]{:S(2)}, u32[]{:S(2)}) collective-permute-start(bf16[128,2048]{1,0:T(8,128)(2,1)} %shard_map.117.refs_0_), channel_id=1, source_target_pairs={{0,16},{8,24},{16,32},{24,40},{32,48},{40,56},{48,0},{56,8},{64,80... | collective-permute-start | bytes 1572872 | tf_op jit(solution)/shard_map/ppermute | solution.py:25
  102.6 23.3 %collective-permute-start.19 = (bf16[128,2048]{1,0:T(8,128)(2,1)}, bf16[128,2048]{1,0:T(8,128)(2,1)S(1)}, u32[]{:S(2)}, u32[]{:S(2)}) collective-permute-start(bf16[128,2048]{1,0:T(8,128)(2,1)} %shard_map.117.refs_0_), channel_id=1, source_target_pairs={{0,48},{8,56},{16,0},{24,8},{32,16},{40,24},{48,32},{56,40},{64,11... | collective-permute-start | bytes 1572872 | tf_op jit(solution)/shard_map/ppermute | solution.py:25
  129.0 12.3 %copy-start.2 = (bf16[512,1024]{1,0:T(8,128)(2,1)S(1)}, bf16[512,1024]{1,0:T(8,128)(2,1)}, u32[]{:S(2)}) copy-start(bf16[512,1024]{1,0:T(8,128)(2,1)} %get-tuple-element.7.refs_3_.refs_2_.hidden_ref) | copy-start | bytes 3145732
  131.3 15.6 %collective-permute-start.22 = (bf16[384,2048]{1,0:T(8,128)(2,1)}, bf16[384,2048]{1,0:T(8,128)(2,1)}, u32[]{:S(2)}, u32[]{:S(2)}) collective-permute-start(bf16[384,2048]{1,0:T(8,128)(2,1)} %shard_map.118), channel_id=1, source_target_pairs={{0,8},{8,0},{16,24},{24,16},{32,40},{40,32},{48,56},{56,48},{64,72... | collective-permute-start | bytes 4718600 | tf_op jit(solution)/shard_map/ppermute | solution.py:25
  132.0 9.2 %collective-permute-start.20 = (bf16[64,2048]{1,0:T(8,128)(2,1)S(1)}, bf16[64,2048]{1,0:T(8,128)(2,1)S(1)}, u32[]{:S(2)}, u32[]{:S(2)}) collective-permute-start(bf16[64,2048]{1,0:T(8,128)(2,1)S(1)} %slice.32), channel_id=1, source_target_pairs={{0,16},{8,24},{16,32},{24,40},{32,48},{40,56},{48,0},{56,8},{64,80... | collective-permute-start | bytes 786440 | tf_op jit(solution)/shard_map/ppermute | solution.py:25
  132.3 8.9 %collective-permute-start.21 = (bf16[64,2048]{1,0:T(8,128)(2,1)S(1)}, bf16[64,2048]{1,0:T(8,128)(2,1)S(1)}, u32[]{:S(2)}, u32[]{:S(2)}) collective-permute-start(bf16[64,2048]{1,0:T(8,128)(2,1)S(1)} %slice.33), channel_id=1, source_target_pairs={{0,48},{8,56},{16,0},{24,8},{32,16},{40,24},{48,32},{56,40},{64,11... | collective-permute-start | bytes 786440 | tf_op jit(solution)/shard_map/ppermute | solution.py:25
  142.2 4.7 %collective-permute-start.23 = (bf16[128,2048]{1,0:T(8,128)(2,1)}, bf16[128,2048]{1,0:T(8,128)(2,1)}, u32[]{:S(2)}, u32[]{:S(2)}) collective-permute-start(bf16[128,2048]{1,0:T(8,128)(2,1)} %shard_map.119), channel_id=1, source_target_pairs={{0,8},{8,0},{16,24},{24,16},{32,40},{40,32},{48,56},{56,48},{64,72... | collective-permute-start | bytes 1572872 | tf_op jit(solution)/shard_map/ppermute | solution.py:25
  143.9 15.2 %collective-permute-start.24 = (bf16[128,2048]{1,0:T(8,128)(2,1)}, bf16[128,2048]{1,0:T(8,128)(2,1)}, u32[]{:S(2)}, u32[]{:S(2)}) collective-permute-start(bf16[128,2048]{1,0:T(8,128)(2,1)} %shard_map.121.refs_0_), channel_id=1, source_target_pairs={{0,16},{8,24},{16,32},{24,40},{32,48},{40,56},{48,0},{56,8},{64,80... | collective-permute-start | bytes 1572872 | tf_op jit(solution)/shard_map/ppermute | solution.py:25
  143.9 15.2 %collective-permute-start.25 = (bf16[128,2048]{1,0:T(8,128)(2,1)}, bf16[128,2048]{1,0:T(8,128)(2,1)}, u32[]{:S(2)}, u32[]{:S(2)}) collective-permute-start(bf16[128,2048]{1,0:T(8,128)(2,1)} %shard_map.121.refs_0_), channel_id=1, source_target_pairs={{0,48},{8,56},{16,0},{24,8},{32,16},{40,24},{48,32},{56,40},{64,11... | collective-permute-start | bytes 1572872 | tf_op jit(solution)/shard_map/ppermute | solution.py:25
  153.9 32.4 %all-to-all-start.2 = ((bf16[8,528,256]{2,1,0:T(8,128)(2,1)}), bf16[8,528,256]{2,1,0:T(8,128)(2,1)}, u32[]{:S(2)}, u32[]{:S(2)}) async-start(bf16[8,528,256]{2,1,0:T(8,128)(2,1)} %shard_map.120.refs_3_.refs_2_), calls=%async_computation.2 | async-start | bytes 4325376 | tf_op jit(solution)/shard_map/all_to_all | solution.py:457
  160.5 14.5 %collective-permute-start.28 = (bf16[384,2048]{1,0:T(8,128)(2,1)S(1)}, bf16[384,2048]{1,0:T(8,128)(2,1)S(1)}, u32[]{:S(2)}, u32[]{:S(2)}) collective-permute-start(bf16[384,2048]{1,0:T(8,128)(2,1)S(1)} %shard_map.122), channel_id=1, source_target_pairs={{0,8},{8,0},{16,24},{24,16},{32,40},{40,32},{48,56},{56,48},{64,72... | collective-permute-start | bytes 4718600 | tf_op jit(solution)/shard_map/ppermute | solution.py:25
  162.3 9.4 %collective-permute-start.26 = (bf16[64,2048]{1,0:T(8,128)(2,1)S(1)}, bf16[64,2048]{1,0:T(8,128)(2,1)S(1)}, u32[]{:S(2)}, u32[]{:S(2)}) collective-permute-start(bf16[64,2048]{1,0:T(8,128)(2,1)S(1)} %slice.37), channel_id=1, source_target_pairs={{0,16},{8,24},{16,32},{24,40},{32,48},{40,56},{48,0},{56,8},{64,80... | collective-permute-start | bytes 786440 | tf_op jit(solution)/shard_map/ppermute | solution.py:25
  164.2 7.8 %collective-permute-start.27 = (bf16[64,2048]{1,0:T(8,128)(2,1)S(1)}, bf16[64,2048]{1,0:T(8,128)(2,1)S(1)}, u32[]{:S(2)}, u32[]{:S(2)}) collective-permute-start(bf16[64,2048]{1,0:T(8,128)(2,1)S(1)} %slice.38), channel_id=1, source_target_pairs={{0,48},{8,56},{16,0},{24,8},{32,16},{40,24},{48,32},{56,40},{64,11... | collective-permute-start | bytes 786440 | tf_op jit(solution)/shard_map/ppermute | solution.py:25
  172.2 2.8 %collective-permute-start.29 = (bf16[128,2048]{1,0:T(8,128)(2,1)S(1)}, bf16[128,2048]{1,0:T(8,128)(2,1)S(1)}, u32[]{:S(2)}, u32[]{:S(2)}) collective-permute-start(bf16[128,2048]{1,0:T(8,128)(2,1)S(1)} %shard_map.123), channel_id=1, source_target_pairs={{0,8},{8,0},{16,24},{24,16},{32,40},{40,32},{48,56},{56,48},{64,72... | collective-permute-start | bytes 1572872 | tf_op jit(solution)/shard_map/ppermute | solution.py:25
  186.3 34.6 %all-to-all-start.3 = ((bf16[8,512,256]{2,1,0:T(8,128)(2,1)}), bf16[8,512,256]{2,1,0:T(8,128)(2,1)S(1)}, u32[]{:S(2)}, u32[]{:S(2)}) async-start(bf16[8,512,256]{2,1,0:T(8,128)(2,1)} %shard_map.124), calls=%async_computation.3 | async-start | bytes 4194304 | tf_op jit(solution)/shard_map/all_to_all | solution.py:457
  (17 other events, 30.6 us)
where the time goes:
time: 223 us; the launch traced here: 222 us
  waiting for transfers between devices  102 us (46%)
  starting transfers between devices  63.8 us (29%)
  Pallas kernels  38.3 us (17%)
  local copies, waits for them, and re-layouts  14.7 us (7%)
  other arithmetic  3.49 us (2%)
    ppermute x23, waiting for transfers between devices, move_rep(): return lax.ppermute(v, 'rep', perm)  35.7 us
    ppermute x23, starting transfers between devices, move_rep(): return lax.ppermute(v, 'rep', perm)  34.2 us
    all_to_all x2, waiting for transfers between devices, per_device(): sums.append(lax.all_to_all(partial, 'tp', 0, 0, tiled=True))  30.6 us
    ppermute x7, waiting for transfers between devices, move_tp(): return lax.ppermute(v, 'tp', perm)  29.4 us
    unnamed x65, local copies, waits for them, and re-layouts  12.7 us
    all_to_all x2, starting transfers between devices, per_device(): sums.append(lax.all_to_all(partial, 'tp', 0, 0, tiled=True))  12.1 us
    pallas_call x1, Pallas kernels, out_product(): pl.pallas_call(kernel, out_shape=[jax.ShapeDtypeStruct((rows, 1024), bf16...  10.6 us
    pallas_call x9, Pallas kernels, concat(): pl.pallas_call(kernel, out_shape=jax.ShapeDtypeStruct((total, cols), bf16...  10.4 us
  transfers between devices with their start and end apart: 34, of which 17 were waited for; matrix products, arithmetic and copies ran while one was open for 2% of the time, Pallas kernels for 15%

commit v1 on v0

--- a/solution.py
+++ b/solution.py
@@ -77,6 +77,19 @@
     )(*[a for a, _ in pieces], *gates)
 
 
+def fence(values, gates=()):
+    def kernel(*refs):
+        pass
+
+    return pl.pallas_call(
+        kernel,
+        out_shape=[jax.ShapeDtypeStruct(v.shape, v.dtype) for v in values],
+        in_specs=[ANY] * (len(values) + len(gates)),
+        out_specs=[ANY] * len(values),
+        input_output_aliases={i: i for i in range(len(values))},
+    )(*values, *gates)
+
+
 def pack_held(ids, out_held, query_held):
     def kernel(ids_ref, out_held_ref, query_held_ref, out_ref):
         turned = out_held_ref[...].astype(f32).T.astype(bf16)
@@ -223,13 +236,13 @@
     )(ids, residual, residual, gain, gain, *gates)
 
 
-def out_product(ids, att, weights, packed):
+def out_product(att, weights):
     copies = [(n, i, g) for n, (_, groups) in enumerate(weights) for i, g in enumerate(groups)]
     rows = att[0].shape[0]
 
-    def kernel(ids_ref, *refs):
-        pieces, w_refs, packed_ref = refs[:8], refs[8 : 8 + len(weights)], refs[8 + len(weights)]
-        hidden_ref, squares_ref, att_buf, w_buf, res_buf, sems = refs[-6:]
+    def kernel(*refs):
+        pieces, w_refs = refs[:8], refs[8 : 8 + len(weights)]
+        out_ref, att_buf, w_buf, sems = refs[-4:]
         waits = []
         for k in range(8):
             lanes = pl.ds(k * 512, 512)
@@ -245,10 +258,6 @@
             for copy in pair:
                 copy.start()
             waits.append(pair)
-        last = pltpu.make_async_copy(
-            packed_ref, res_buf, sems.at[8, 0]
-        )
-        last.start()
         total = None
         for k in range(8):
             for copy in waits[k]:
@@ -257,7 +266,27 @@
                 att_buf[k], w_buf[k], NT, preferred_element_type=f32
             )
             total = product if total is None else total + product
-        last.wait()
+        out_ref[...] = total
+
+    return pl.pallas_call(
+        kernel,
+        out_shape=jax.ShapeDtypeStruct((rows, 1024), f32),
+        in_specs=[ANY] * (8 + len(weights)),
+        out_specs=pl.BlockSpec(memory_space=pltpu.VMEM),
+        scratch_shapes=[
+            pltpu.VMEM((8, rows, 512), bf16),
+            pltpu.VMEM((8, 1024, 512), bf16),
+            pltpu.SemaphoreType.DMA((8, 17)),
+        ],
+        compiler_params=LIMIT,
+        cost_estimate=cost(14, 2 * rows * 4096 * 1024),
+    )(*att, *[v for v, _ in weights])
+
+
+def add_residual(ids, mixture, packed):
+    rows = mixture.shape[0]
+
+    def kernel(ids_ref, mixture_ref, res_ref, hidden_ref, squares_ref):
         major, minor = ids_ref[0] // 8, lax.rem(ids_ref[0] // 2, 4)
         squares = jnp.zeros((rows, 128), f32)
         for part in range(2):
@@ -266,14 +295,17 @@
                 residual, gain = [], []
                 for d in range(2):
                     group = relative(jnp.int32(g + d), major, minor)
-                    residual.append(res_buf[group, :rows, :].astype(f32)[:, lanes])
-                    three = res_buf[group, rows:, :].astype(f32)[:, lanes]
+                    residual.append(res_ref[group, :rows, :].astype(f32)[:, lanes])
+                    three = res_ref[group, rows:, :].astype(f32)[:, lanes]
                     gain.append(three[0:1] + three[1:2] + three[2:3])
                 at = slice(part * 512 + g * 64, part * 512 + g * 64 + 128)
-                updated = total[:, at] + jnp.concatenate(residual, axis=1)
+                updated = mixture_ref[:, at] + jnp.concatenate(residual, axis=1)
                 hidden_ref[:, at] = (updated * jnp.concatenate(gain, axis=1)).astype(bf16)
                 squares = squares + updated * updated
         squares_ref[...] = squares
+
+    def whole(*shape):
+        return pl.BlockSpec(shape, lambda i, ids: (0,) * len(shape))
 
     return pl.pallas_call(
         kernel,
@@ -284,21 +316,12 @@
         grid_spec=pltpu.PrefetchScalarGridSpec(
             num_scalar_prefetch=1,
             grid=(1,),
-            in_specs=[ANY] * (9 + len(weights)),
-            out_specs=[
-                pl.BlockSpec((rows, 1024), lambda i, ids: (0, 0)),
-                pl.BlockSpec((rows, 128), lambda i, ids: (0, 0)),
-            ],
-            scratch_shapes=[
-                pltpu.VMEM((8, rows, 512), bf16),
-                pltpu.VMEM((8, 1024, 512), bf16),
-                pltpu.VMEM((8, rows + 16, 128), bf16),
-                pltpu.SemaphoreType.DMA((9, 17)),
-            ],
+            in_specs=[whole(rows, 1024), whole(8, rows + 16, 128)],
+            out_specs=[whole(rows, 1024), whole(rows, 128)],
         ),
         compiler_params=LIMIT,
-        cost_estimate=cost(14, 2 * rows * 4096 * 1024),
-    )(ids, *att, *[v for v, _ in weights], packed)
+        cost_estimate=cost(4),
+    )(ids, mixture, packed)
 
 
 def query_product(hidden, weights, extra):
@@ -404,9 +427,10 @@
     )
     packed = lax.all_to_all(packed, "tp", 0, 0, tiled=True)
 
-    f_own = move_rep(l_own, dx=1)
     l_par = move_rep(par, dx=1)
     r_par = move_rep(par, dx=-1)
+    l_own, r_par = fence((l_own, r_par), (l_par,))
+    f_own = move_rep(l_own, dx=1)
     first = concat(
         [(v, None) for v in (own, par, l_own, r_own)], (a_f_own, a_l_par, a_r_par, blocks_par)
     )
@@ -427,7 +451,7 @@
         (move_rep(f_par, dc=1), (15,)),
     ]
 
-    hidden, squares = out_product(ids, att, weights, packed)
+    hidden, squares = add_residual(ids, out_product(att, weights), packed)
     squares = jnp.stack(split3(jnp.sum(squares, axis=1))).reshape(3 * rows // w, w)
     squares = jnp.concatenate([squares, jnp.zeros((16 - 3 * rows // w, w), bf16)], axis=0)
 

time: 223 us -> 216 us (0.969)
  waiting for transfers between devices: 102 us -> 93.8 us
  local copies, waits for them, and re-layouts: 14.7 us -> 12.2 us
    all_to_all x1, waiting for transfers between devices: 5.78 us -> 0.01 us  [per_device(): packed = lax.all_to_all(packed, 'tp', 0, 0, tiled=True)]
    ppermute x23, waiting for transfers between devices: 35.7 us -> 31.8 us  [move_rep(): return lax.ppermute(v, 'rep', perm)]
    all_to_all x1, starting transfers between devices: 4.19 us -> 6.52 us  [per_device(): held = lax.all_to_all(held, 'tp', 0, 0, tiled=True)]
    unnamed x65 -> x61, local copies, waits for them, and re-layouts: 12.7 us -> 11.2 us
    pallas_call x1 -> x3, Pallas kernels: 10.6 us -> 12.1 us  [the longest x1 9.46 us: out_product(): pl.pallas_call(kernel, out_shape=jax.ShapeDtypeStruct((rows, 1024), f32),...]
  transfers between devices with their start and end apart: 34 -> 34, of which waited for: 17 -> 14; matrix products, arithmetic and copies ran while one was open for 2% -> 2% of each run, Pallas kernels for 15% -> 15%
where the time goes in v1:
time: 216 us; the launch traced here: 215 us
  waiting for transfers between devices  93.8 us (43%)
  starting transfers between devices  65.8 us (30%)
  Pallas kernels  38.9 us (18%)
  local copies, waits for them, and re-layouts  12.2 us (6%)
  other arithmetic  3.49 us (2%)
    ppermute x23, starting transfers between devices, move_rep(): return lax.ppermute(v, 'rep', perm)  33.1 us
    all_to_all x2, waiting for transfers between devices, per_device(): sums.append(lax.all_to_all(partial, 'tp', 0, 0, tiled=True))  32.1 us
    ppermute x23, waiting for transfers between devices, move_rep(): return lax.ppermute(v, 'rep', perm)  31.8 us
    ppermute x7, waiting for transfers between devices, move_tp(): return lax.ppermute(v, 'tp', perm)  30 us
    all_to_all x2, starting transfers between devices, per_device(): sums.append(lax.all_to_all(partial, 'tp', 0, 0, tiled=True))  12 us
    unnamed x61, local copies, waits for them, and re-layouts  11.2 us
    pallas_call x9, Pallas kernels, concat(): pl.pallas_call(kernel, out_shape=jax.ShapeDtypeStruct((total, cols), bf16...  10.7 us
    ppermute x7, starting transfers between devices, move_tp(): return lax.ppermute(v, 'tp', perm)  9.88 us
  transfers between devices with their start and end apart: 34, of which 14 were waited for; matrix products, arithmetic and copies ran while one was open for 2% of the time, Pallas kernels for 15%

profile of v1, /device:TPU:1, one launch (start us, length us, event | category | flops | bytes accessed | tf_op | source)
XLA Modules:
  0.0 214.7 jit_solution(5279751008789588590)
XLA Ops:
  0.1 2.7 %shard_map.109.refs_1_ = bf16[8,64,1024]{2,1,0:T(8,128)(2,1)} custom-call(s32[2]{0:T(128)S(1)} %pad_add_fusion.ids_ref, bf16[512,8192]{1,0:T(8,128)(2,1)} %out_held_ref.1, bf16[8192,512]{1,0:T(8,128)(2,1)} %query_held_ref.1), custom_call_target="tpu_custom_call" | custom-call | bytes 2097152 | tf_op jit(solution)/shard_map/pallas_call | solution.py:99
  2.8 6.5 %all-to-all-start = ((bf16[8,64,1024]{2,1,0:T(8,128)(2,1)}), bf16[8,64,1024]{2,1,0:T(8,128)(2,1)S(1)}, u32[]{:S(2)}, u32[]{:S(2)}) async-start(bf16[8,64,1024]{2,1,0:T(8,128)(2,1)} %shard_map.109.refs_1_), calls=%async_computation | async-start | bytes 2097152 | tf_op jit(solution)/shard_map/all_to_all | solution.py:406
  9.4 1.5 collective-permute-start
  10.9 1.2 collective-permute-start.1
  12.1 1.5 collective-permute-start.3
  14.4 19.0 %collective-permute-done.rest_0_.refs_1_ = bf16[512,512]{1,0:T(8,128)(2,1)} collective-permute-done((bf16[512,512]{1,0:T(8,128)(2,1)S(1)}, bf16[512,512]{1,0:T(8,128)(2,1)}, u32[]{:S(2)}, u32[]{:S(2)}) %collective-permute-start) | collective-permute-done | bytes 524320 | tf_op jit(solution)/shard_map/ppermute | solution.py:33
  33.4 2.2 %collective-permute-done.1.rest_1_.refs_2_ = bf16[512,512]{1,0:T(8,128)(2,1)} collective-permute-done((bf16[512,512]{1,0:T(8,128)(2,1)S(1)}, bf16[512,512]{1,0:T(8,128)(2,1)}, u32[]{:S(2)}, u32[]{:S(2)}) %collective-permute-start.1) | collective-permute-done | bytes 524320 | tf_op jit(solution)/shard_map/ppermute | solution.py:33
  37.5 1.2 shard_map.111.rest_0_.refs_0_.refs_8_
  38.7 3.4 %collective-permute-start.7 = (bf16[64,4096]{1,0:T(8,128)(2,1)S(1)}, bf16[64,4096]{1,0:T(8,128)(2,1)}, u32[]{:S(2)}, u32[]{:S(2)}) collective-permute-start(bf16[64,4096]{1,0:T(8,128)(2,1)S(1)} %shard_map.111.rest_0_.refs_0_.refs_8_), channel_id=1, source_target_pairs={{0,64},{8,72},{16,80},{24,88},{32,96},{40,104},{48,112},{56,120},{... | collective-permute-start | bytes 1572872 | tf_op jit(solution)/shard_map/ppermute | solution.py:25
  42.1 1.5 collective-permute-start.4
  43.6 1.2 collective-permute-start.8
  44.8 8.8 %collective-permute-done.7.refs_1_.refs_9_ = bf16[64,4096]{1,0:T(8,128)(2,1)} collective-permute-done((bf16[64,4096]{1,0:T(8,128)(2,1)S(1)}, bf16[64,4096]{1,0:T(8,128)(2,1)}, u32[]{:S(2)}, u32[]{:S(2)}) %collective-permute-start.7) | collective-permute-done | bytes 524320 | tf_op jit(solution)/shard_map/ppermute | solution.py:25
  53.6 2.5 %collective-permute-start.9 = (bf16[64,4096]{1,0:T(8,128)(2,1)}, bf16[64,4096]{1,0:T(8,128)(2,1)S(1)}, u32[]{:S(2)}, u32[]{:S(2)}) collective-permute-start(bf16[64,4096]{1,0:T(8,128)(2,1)} %collective-permute-done.7.refs_1_.refs_9_), channel_id=1, source_target_pairs={{0,48},{8,56},{16,0},{24,8},{32,16},{40,24},{48,32},{56,40},{64,11... | collective-permute-start | bytes 1572872 | tf_op jit(solution)/shard_map/ppermute | solution.py:25
  56.3 1.2 copy-done.12
  58.6 1.4 shard_map.113.refs_0_
  60.0 1.9 collective-permute-start.5
  61.9 2.7 %collective-permute-start.11 = (bf16[64,4096]{1,0:T(8,128)(2,1)S(1)}, bf16[64,4096]{1,0:T(8,128)(2,1)}, u32[]{:S(2)}, u32[]{:S(2)}) collective-permute-start(bf16[64,4096]{1,0:T(8,128)(2,1)S(1)} %shard_map.111.rest_0_.refs_0_.refs_8_), channel_id=1, source_target_pairs={{0,48},{8,56},{16,0},{24,8},{32,16},{40,24},{48,32},{56,40},{64,11... | collective-permute-start | bytes 1572872 | tf_op jit(solution)/shard_map/ppermute | solution.py:25
  64.6 1.6 collective-permute-done.9.refs_1_
  66.2 2.3 %collective-permute-start.14 = (bf16[2,64,2048]{2,1,0:T(8,128)(2,1)S(1)}, bf16[2,64,2048]{2,1,0:T(8,128)(2,1)S(1)}, u32[]{:S(2)}, u32[]{:S(2)}) collective-permute-start(bf16[2,64,2048]{2,1,0:T(8,128)(2,1)S(1)} %shard_map.113.refs_0_), channel_id=1, source_target_pairs={{0,64},{8,72},{16,80},{24,88},{32,96},{40,104},{48,112},{56,120},{... | collective-permute-start | bytes 1572872 | tf_op jit(solution)/shard_map/ppermute | solution.py:25
  69.5 2.2 %collective-permute-start.6 = (bf16[512,512]{1,0:T(8,128)(2,1)}, bf16[512,512]{1,0:T(8,128)(2,1)}, u32[]{:S(2)}, u32[]{:S(2)}) collective-permute-start(bf16[512,512]{1,0:T(8,128)(2,1)} %collective-permute-done.4.refs_6_.refs_5_), channel_id=1, source_target_pairs={{0,3},{1,0},{2,1},{3,2},{4,7},{5,4},{6,5},{7,6},{8,11},{9,8},{10,9... | collective-permute-start | bytes 1572872 | tf_op jit(solution)/shard_map/ppermute | solution.py:33
  71.9 8.8 %collective-permute-done.5.refs_4_.refs_6_ = bf16[512,512]{1,0:T(8,128)(2,1)} collective-permute-done((bf16[512,512]{1,0:T(8,128)(2,1)}, bf16[512,512]{1,0:T(8,128)(2,1)}, u32[]{:S(2)}, u32[]{:S(2)}) %collective-permute-start.5) | collective-permute-done | bytes 524320 | tf_op jit(solution)/shard_map/ppermute | solution.py:33
  80.7 2.6 %shard_map.114 = bf16[256,4096]{1,0:T(8,128)(2,1)} custom-call(bf16[64,4096]{1,0:T(8,128)(2,1)S(1)} %shard_map.111.rest_0_.refs_0_.refs_8_, bf16[64,4096]{1,0:T(8,128)(2,1)} %collective-permute-done.7.refs_1_.refs_9_, bf16[64,4096]{1,0:T(8,128)(2,1)} %get-tuple-element.9.refs_2_.refs_10_, bf16[64,4096]{1,0:T(8,128)(2,1)} %collective-permute-done.11.refs_3_.refs_12_, ...), custom_call_target="tpu_custom_call" | custom-call | bytes 4194304 | tf_op jit(solution)/shard_map/pallas_call | solution.py:69
  83.3 2.6 %collective-permute-start.15 = (bf16[256,4096]{1,0:T(8,128)(2,1)}, bf16[256,4096]{1,0:T(8,128)(2,1)}, u32[]{:S(2)}, u32[]{:S(2)}) collective-permute-start(bf16[256,4096]{1,0:T(8,128)(2,1)} %shard_map.114), channel_id=1, source_target_pairs={{0,8},{8,0},{16,24},{24,16},{32,40},{40,32},{48,56},{56,48},{64,72... | collective-permute-start | bytes 6291464 | tf_op jit(solution)/shard_map/ppermute | solution.py:25
  86.0 1.4 shard_map.115
  87.4 1.7 collective-permute-start.16
  89.0 1.2 collective-permute-start.13
  92.3 4.3 %all-to-all-start.1 = ((bf16[8,528,128]{2,1,0:T(8,128)(2,1)}), bf16[8,528,128]{2,1,0:T(8,128)(2,1)}, u32[]{:S(2)}, u32[]{:S(2)}) async-start(bf16[8,528,128]{2,1,0:T(8,128)(2,1)} %copy-done.5), calls=%async_computation.1 | async-start | bytes 2162688 | tf_op jit(solution)/shard_map/all_to_all | solution.py:428
  96.6 6.1 %collective-permute-done.13.refs_15_ = bf16[64,4096]{1,0:T(8,128)(2,1)} collective-permute-done((bf16[64,4096]{1,0:T(8,128)(2,1)S(1)}, bf16[64,4096]{1,0:T(8,128)(2,1)}, u32[]{:S(2)}, u32[]{:S(2)}) %collective-permute-start.13) | collective-permute-done | bytes 524320 | tf_op jit(solution)/shard_map/ppermute | solution.py:25
  104.4 2.7 %collective-permute-start.19 = (bf16[128,2048]{1,0:T(8,128)(2,1)}, bf16[128,2048]{1,0:T(8,128)(2,1)S(1)}, u32[]{:S(2)}, u32[]{:S(2)}) collective-permute-start(bf16[128,2048]{1,0:T(8,128)(2,1)} %shard_map.119.refs_0_), channel_id=1, source_target_pairs={{0,48},{8,56},{16,0},{24,8},{32,16},{40,24},{48,32},{56,40},{64,11... | collective-permute-start | bytes 1572872 | tf_op jit(solution)/shard_map/ppermute | solution.py:25
  107.9 9.5 %shard_map.116.mixture_ref = f32[512,1024]{1,0:T(8,128)} custom-call(bf16[512,512]{1,0:T(8,128)(2,1)S(1)} %copy-done.20, bf16[512,512]{1,0:T(8,128)(2,1)} %collective-permute-done.rest_0_.refs_1_, bf16[512,512]{1,0:T(8,128)(2,1)} %collective-permute-done.1.rest_1_.refs_2_, bf16[512,512]{1,0:T(8,128)(2,1)} %collective-permute-done.2.refs_5_.refs_3_, ...), custom_call_target="tpu_custom_call" | custom-call | flops 4294967296 | bytes 14680064 | tf_op jit(solution)/shard_map/pallas_call | solution.py:271
  117.4 1.6 copy-done.9
  119.0 2.7 %shard_map.118 = (bf16[512,1024]{1,0:T(8,128)(2,1)S(1)}, f32[512,128]{1,0:T(8,128)S(1)}) custom-call(s32[2]{0:T(128)S(1)} %pad_add_fusion.ids_ref, f32[512,1024]{1,0:T(8,128)S(1)} %copy-done.9, bf16[8,528,128]{2,1,0:T(8,128)(2,1)} %all-to-all-done.1.res_ref), custom_call_target="tpu_custom_call" | custom-call | bytes 4194304 | tf_op jit(solution)/shard_map/pallas_call | solution.py:310
  121.7 2.4 %shard_map.120 = bf16[384,2048]{1,0:T(8,128)(2,1)} custom-call(bf16[128,2048]{1,0:T(8,128)(2,1)} %shard_map.119.refs_0_, bf16[128,2048]{1,0:T(8,128)(2,1)S(1)} %collective-permute-done.18.refs_1_.refs_2_, bf16[128,2048]{1,0:T(8,128)(2,1)S(1)} %collective-permute-done.19.refs_2_.refs_3_, bf16[512,1024]{1,0:T(8,128)(2,1)S(1)} %get-tuple-element.11.refs_3_.refs_2_.hidden_ref), custom_call_target="tpu_custom_call" | custom-call | bytes 3145728 | tf_op jit(solution)/shard_map/pallas_call | solution.py:69
  124.7 2.7 %collective-permute-start.21 = (bf16[64,2048]{1,0:T(8,128)(2,1)S(1)}, bf16[64,2048]{1,0:T(8,128)(2,1)S(1)}, u32[]{:S(2)}, u32[]{:S(2)}) collective-permute-start(bf16[64,2048]{1,0:T(8,128)(2,1)S(1)} %slice.33), channel_id=1, source_target_pairs={{0,48},{8,56},{16,0},{24,8},{32,16},{40,24},{48,32},{56,40},{64,11... | collective-permute-start | bytes 786440 | tf_op jit(solution)/shard_map/ppermute | solution.py:25
  127.5 6.4 %collective-permute-done.20.refs_0_.refs_3_ = bf16[64,2048]{1,0:T(8,128)(2,1)S(1)} collective-permute-done((bf16[64,2048]{1,0:T(8,128)(2,1)S(1)}, bf16[64,2048]{1,0:T(8,128)(2,1)S(1)}, u32[]{:S(2)}, u32[]{:S(2)}) %collective-permute-start.20) | collective-permute-done | bytes 262176 | tf_op jit(solution)/shard_map/ppermute | solution.py:25
  136.5 2.8 %collective-permute-start.25 = (bf16[128,2048]{1,0:T(8,128)(2,1)}, bf16[128,2048]{1,0:T(8,128)(2,1)}, u32[]{:S(2)}, u32[]{:S(2)}) collective-permute-start(bf16[128,2048]{1,0:T(8,128)(2,1)} %shard_map.123.refs_0_), channel_id=1, source_target_pairs={{0,48},{8,56},{16,0},{24,8},{32,16},{40,24},{48,32},{56,40},{64,11... | collective-permute-start | bytes 1572872 | tf_op jit(solution)/shard_map/ppermute | solution.py:25
  141.4 5.1 %shard_map.122.refs_3_.refs_2_ = bf16[8,528,256]{2,1,0:T(8,128)(2,1)} custom-call(bf16[512,1024]{1,0:T(8,128)(2,1)S(1)} %get-tuple-element.11.refs_3_.refs_2_.hidden_ref, bf16[128,2048]{1,0:T(8,128)(2,1)} %shard_map.119.refs_0_, bf16[128,2048]{1,0:T(8,128)(2,1)S(1)} %collective-permute-done.18.refs_1_.refs_2_, ...), custom_call_target="tpu_custom_call" | custom-call | flops 2147483648 | bytes 8388608 | tf_op jit(solution)/shard_map/pallas_call | solution.py:361
  146.5 4.5 %all-to-all-start.2 = ((bf16[8,528,256]{2,1,0:T(8,128)(2,1)}), bf16[8,528,256]{2,1,0:T(8,128)(2,1)}, u32[]{:S(2)}, u32[]{:S(2)}) async-start(bf16[8,528,256]{2,1,0:T(8,128)(2,1)} %shard_map.122.refs_3_.refs_2_), calls=%async_computation.2 | async-start | bytes 4325376 | tf_op jit(solution)/shard_map/all_to_all | solution.py:481
  151.5 1.3 shard_map.124
  155.7 1.9 collective-permute-start.27
  157.7 5.6 %collective-permute-done.26.refs_0_.refs_3_ = bf16[64,2048]{1,0:T(8,128)(2,1)S(1)} collective-permute-done((bf16[64,2048]{1,0:T(8,128)(2,1)S(1)}, bf16[64,2048]{1,0:T(8,128)(2,1)S(1)}, u32[]{:S(2)}, u32[]{:S(2)}) %collective-permute-start.26) | collective-permute-done | bytes 262176 | tf_op jit(solution)/shard_map/ppermute | solution.py:25
  163.7 1.1 collective-permute-start.29
  164.8 1.5 collective-permute-done.29.refs_6_
  166.3 4.6 %shard_map.126 = bf16[8,512,256]{2,1,0:T(8,128)(2,1)} custom-call(bf16[512,1024]{1,0:T(8,128)(2,1)S(1)} %copy-done.7, bf16[128,2048]{1,0:T(8,128)(2,1)} %shard_map.123.refs_0_, bf16[128,2048]{1,0:T(8,128)(2,1)S(1)} %collective-permute-done.24.refs_1_, bf16[128,2048]{1,0:T(8,128)(2,1)} %collective-permute-done.25.refs_2_, ...), custom_call_target="tpu_custom_call" | custom-call | flops 2147483648 | bytes 8388608 | tf_op jit(solution)/shard_map/pallas_call | solution.py:361
  171.0 7.9 %all-to-all-done.2 = bf16[8,528,256]{2,1,0:T(8,128)(2,1)} async-done(((bf16[8,528,256]{2,1,0:T(8,128)(2,1)}), bf16[8,528,256]{2,1,0:T(8,128)(2,1)}, u32[]{:S(2)}, u32[]{:S(2)}) %all-to-all-start.2) | async-done | bytes 2162720 | tf_op jit(solution)/shard_map/all_to_all | solution.py:481
  178.9 7.5 %all-to-all-start.3 = ((bf16[8,512,256]{2,1,0:T(8,128)(2,1)}), bf16[8,512,256]{2,1,0:T(8,128)(2,1)S(1)}, u32[]{:S(2)}, u32[]{:S(2)}) async-start(bf16[8,512,256]{2,1,0:T(8,128)(2,1)} %shard_map.126), calls=%async_computation.3 | async-start | bytes 4194304 | tf_op jit(solution)/shard_map/all_to_all | solution.py:481
  187.3 1.9 convert_reduce_fusion.1
  189.2 24.2 %all-to-all-done.3 = bf16[8,512,256]{2,1,0:T(8,128)(2,1)S(1)} async-done(((bf16[8,512,256]{2,1,0:T(8,128)(2,1)}), bf16[8,512,256]{2,1,0:T(8,128)(2,1)S(1)}, u32[]{:S(2)}, u32[]{:S(2)}) %all-to-all-start.3) | async-done | bytes 2097184 | tf_op jit(solution)/shard_map/all_to_all | solution.py:481
  (118 shorter events, 21.0 us)
Async XLA Ops:
  2.8 6.5 %copy-start.17 = (bf16[4,128,512]{2,1,0:T(8,128)(2,1)S(1)}, bf16[4,128,512]{2,1,0:T(8,128)(2,1)}, u32[]{:S(2)}) copy-start(bf16[4,128,512]{2,1,0:T(8,128)(2,1)} %param.19) | copy-start | bytes 1572868
  2.8 33.6 %copy-start.11 = (f32[4096,64]{0,1:T(8,128)S(1)}, f32[4096,64]{0,1:T(8,128)}, u32[]{:S(2)}) copy-start(f32[4096,64]{0,1:T(8,128)} %param.11) | copy-start | bytes 3145732
  2.8 33.6 %copy-start.13 = (bf16[4096,64]{0,1:T(8,128)(2,1)S(1)}, bf16[4096,64]{0,1:T(8,128)(2,1)}, u32[]{:S(2)}) copy-start(bf16[4096,64]{0,1:T(8,128)(2,1)} %param.12) | copy-start | bytes 1572868
  2.8 33.6 %copy-start.25 = (s32[32,64]{1,0:T(8,128)S(1)}, s32[32,64]{1,0:T(8,128)}, u32[]{:S(2)}) copy-start(s32[32,64]{1,0:T(8,128)} %scales_ref.2) | copy-start | bytes 24580
  2.8 33.6 %all-to-all-start = ((bf16[8,64,1024]{2,1,0:T(8,128)(2,1)}), bf16[8,64,1024]{2,1,0:T(8,128)(2,1)S(1)}, u32[]{:S(2)}, u32[]{:S(2)}) async-start(bf16[8,64,1024]{2,1,0:T(8,128)(2,1)} %shard_map.109.refs_1_), calls=%async_computation | async-start | bytes 2097152 | tf_op jit(solution)/shard_map/all_to_all | solution.py:406
  9.4 24.0 %collective-permute-start = (bf16[512,512]{1,0:T(8,128)(2,1)S(1)}, bf16[512,512]{1,0:T(8,128)(2,1)}, u32[]{:S(2)}, u32[]{:S(2)}) collective-permute-start(bf16[512,512]{1,0:T(8,128)(2,1)S(1)} %shard_map.110.refs_0_), channel_id=1, source_target_pairs={{0,4},{1,5},{2,6},{3,7},{4,0},{5,1},{6,2},{7,3},{8,12},{9,13},{10,... | collective-permute-start | bytes 1572872 | tf_op jit(solution)/shard_map/ppermute | solution.py:33
  10.9 24.7 %collective-permute-start.1 = (bf16[512,512]{1,0:T(8,128)(2,1)S(1)}, bf16[512,512]{1,0:T(8,128)(2,1)}, u32[]{:S(2)}, u32[]{:S(2)}) collective-permute-start(bf16[512,512]{1,0:T(8,128)(2,1)S(1)} %shard_map.110.refs_0_), channel_id=1, source_target_pairs={{0,1},{1,2},{2,3},{3,0},{4,5},{5,6},{6,7},{7,4},{8,9},{9,10},{10,1... | collective-permute-start | bytes 1572872 | tf_op jit(solution)/shard_map/ppermute | solution.py:33
  12.1 23.5 %collective-permute-start.3 = (bf16[512,512]{1,0:T(8,128)(2,1)S(1)}, bf16[512,512]{1,0:T(8,128)(2,1)S(1)}, u32[]{:S(2)}, u32[]{:S(2)}) collective-permute-start(bf16[512,512]{1,0:T(8,128)(2,1)S(1)} %shard_map.110.refs_0_), channel_id=1, source_target_pairs={{0,3},{1,0},{2,1},{3,2},{4,7},{5,4},{6,5},{7,6},{8,11},{9,8},{10,9... | collective-permute-start | bytes 1572872 | tf_op jit(solution)/shard_map/ppermute | solution.py:33
  37.5 18.6 %copy-start.27 = (s32[64,32]{0,1:T(8,128)S(1)}, s32[64,32]{0,1:T(8,128)}, u32[]{:S(2)}) copy-start(s32[64,32]{0,1:T(8,128)} %param.18) | copy-start | bytes 24580
  38.7 14.9 %collective-permute-start.7 = (bf16[64,4096]{1,0:T(8,128)(2,1)S(1)}, bf16[64,4096]{1,0:T(8,128)(2,1)}, u32[]{:S(2)}, u32[]{:S(2)}) collective-permute-start(bf16[64,4096]{1,0:T(8,128)(2,1)S(1)} %shard_map.111.rest_0_.refs_0_.refs_8_), channel_id=1, source_target_pairs={{0,64},{8,72},{16,80},{24,88},{32,96},{40,104},{48,112},{56,120},{... | collective-permute-start | bytes 1572872 | tf_op jit(solution)/shard_map/ppermute | solution.py:25
  42.1 18.0 %collective-permute-start.4 = (bf16[512,512]{1,0:T(8,128)(2,1)}, bf16[512,512]{1,0:T(8,128)(2,1)}, u32[]{:S(2)}, u32[]{:S(2)}) collective-permute-start(bf16[512,512]{1,0:T(8,128)(2,1)} %collective-permute-done.rest_0_.refs_1_), channel_id=1, source_target_pairs={{0,3},{1,0},{2,1},{3,2},{4,7},{5,4},{6,5},{7,6},{8,11},{9,8},{10,9... | collective-permute-start | bytes 1572872 | tf_op jit(solution)/shard_map/ppermute | solution.py:33
  43.6 18.3 %collective-permute-start.8 = (bf16[64,4096]{1,0:T(8,128)(2,1)S(1)}, bf16[64,4096]{1,0:T(8,128)(2,1)}, u32[]{:S(2)}, u32[]{:S(2)}) collective-permute-start(bf16[64,4096]{1,0:T(8,128)(2,1)S(1)} %shard_map.111.rest_0_.refs_0_.refs_8_), channel_id=1, source_target_pairs={{0,16},{8,24},{16,32},{24,40},{32,48},{40,56},{48,0},{56,8},{64,80... | collective-permute-start | bytes 1572872 | tf_op jit(solution)/shard_map/ppermute | solution.py:25
  53.6 12.6 %collective-permute-start.9 = (bf16[64,4096]{1,0:T(8,128)(2,1)}, bf16[64,4096]{1,0:T(8,128)(2,1)S(1)}, u32[]{:S(2)}, u32[]{:S(2)}) collective-permute-start(bf16[64,4096]{1,0:T(8,128)(2,1)} %collective-permute-done.7.refs_1_.refs_9_), channel_id=1, source_target_pairs={{0,48},{8,56},{16,0},{24,8},{32,16},{40,24},{48,32},{56,40},{64,11... | collective-permute-start | bytes 1572872 | tf_op jit(solution)/shard_map/ppermute | solution.py:25
  56.2 15.6 %collective-permute-start.2 = (bf16[512,512]{1,0:T(8,128)(2,1)}, bf16[512,512]{1,0:T(8,128)(2,1)}, u32[]{:S(2)}, u32[]{:S(2)}) collective-permute-start(bf16[512,512]{1,0:T(8,128)(2,1)} %collective-permute-done.rest_0_.refs_1_), channel_id=1, source_target_pairs={{0,1},{1,2},{2,3},{3,0},{4,5},{5,6},{6,7},{7,4},{8,9},{9,10},{10,1... | collective-permute-start | bytes 1572872 | tf_op jit(solution)/shard_map/ppermute | solution.py:33
  56.2 13.3 %collective-permute-start.10 = (bf16[64,4096]{1,0:T(8,128)(2,1)}, bf16[64,4096]{1,0:T(8,128)(2,1)S(1)}, u32[]{:S(2)}, u32[]{:S(2)}) collective-permute-start(bf16[64,4096]{1,0:T(8,128)(2,1)} %collective-permute-done.7.refs_1_.refs_9_), channel_id=1, source_target_pairs={{0,16},{8,24},{16,32},{24,40},{32,48},{40,56},{48,0},{56,8},{64,80... | collective-permute-start | bytes 1572872 | tf_op jit(solution)/shard_map/ppermute | solution.py:25
  60.0 20.7 %collective-permute-start.5 = (bf16[512,512]{1,0:T(8,128)(2,1)}, bf16[512,512]{1,0:T(8,128)(2,1)}, u32[]{:S(2)}, u32[]{:S(2)}) collective-permute-start(bf16[512,512]{1,0:T(8,128)(2,1)} %collective-permute-done.1.rest_1_.refs_2_), channel_id=1, source_target_pairs={{0,1},{1,2},{2,3},{3,0},{4,5},{5,6},{6,7},{7,4},{8,9},{9,10},{10,1... | collective-permute-start | bytes 1572872 | tf_op jit(solution)/shard_map/ppermute | solution.py:33
  61.9 18.8 %collective-permute-start.11 = (bf16[64,4096]{1,0:T(8,128)(2,1)S(1)}, bf16[64,4096]{1,0:T(8,128)(2,1)}, u32[]{:S(2)}, u32[]{:S(2)}) collective-permute-start(bf16[64,4096]{1,0:T(8,128)(2,1)S(1)} %shard_map.111.rest_0_.refs_0_.refs_8_), channel_id=1, source_target_pairs={{0,48},{8,56},{16,0},{24,8},{32,16},{40,24},{48,32},{56,40},{64,11... | collective-permute-start | bytes 1572872 | tf_op jit(solution)/shard_map/ppermute | solution.py:25
  66.2 14.5 %collective-permute-start.14 = (bf16[2,64,2048]{2,1,0:T(8,128)(2,1)S(1)}, bf16[2,64,2048]{2,1,0:T(8,128)(2,1)S(1)}, u32[]{:S(2)}, u32[]{:S(2)}) collective-permute-start(bf16[2,64,2048]{2,1,0:T(8,128)(2,1)S(1)} %shard_map.113.refs_0_), channel_id=1, source_target_pairs={{0,64},{8,72},{16,80},{24,88},{32,96},{40,104},{48,112},{56,120},{... | collective-permute-start | bytes 1572872 | tf_op jit(solution)/shard_map/ppermute | solution.py:25
  69.5 16.4 %collective-permute-start.6 = (bf16[512,512]{1,0:T(8,128)(2,1)}, bf16[512,512]{1,0:T(8,128)(2,1)}, u32[]{:S(2)}, u32[]{:S(2)}) collective-permute-start(bf16[512,512]{1,0:T(8,128)(2,1)} %collective-permute-done.4.refs_6_.refs_5_), channel_id=1, source_target_pairs={{0,3},{1,0},{2,1},{3,2},{4,7},{5,4},{6,5},{7,6},{8,11},{9,8},{10,9... | collective-permute-start | bytes 1572872 | tf_op jit(solution)/shard_map/ppermute | solution.py:33
  71.8 14.2 %copy-start.2 = (bf16[64,4096]{1,0:T(8,128)(2,1)S(1)}, bf16[64,4096]{1,0:T(8,128)(2,1)}, u32[]{:S(2)}) copy-start(bf16[64,4096]{1,0:T(8,128)(2,1)} %copy-done.1) | copy-start | bytes 1572868
  71.8 14.2 %copy-start.4 = (bf16[64,4096]{1,0:T(8,128)(2,1)S(1)}, bf16[64,4096]{1,0:T(8,128)(2,1)}, u32[]{:S(2)}) copy-start(bf16[64,4096]{1,0:T(8,128)(2,1)} %get-tuple-element.10.refs_1_.refs_13_.refs_3_) | copy-start | bytes 1572868
  71.8 14.1 %collective-permute-start.12 = (bf16[64,4096]{1,0:T(8,128)(2,1)}, bf16[64,4096]{1,0:T(8,128)(2,1)S(1)}, u32[]{:S(2)}, u32[]{:S(2)}) collective-permute-start(bf16[64,4096]{1,0:T(8,128)(2,1)} %get-tuple-element.9.refs_2_.refs_10_), channel_id=1, source_target_pairs={{0,16},{8,24},{16,32},{24,40},{32,48},{40,56},{48,0},{56,8},{64,80... | collective-permute-start | bytes 1572872 | tf_op jit(solution)/shard_map/ppermute | solution.py:25
  83.3 7.0 %copy-start.8 = (bf16[4,128,1024]{2,1,0:T(8,128)(2,1)S(1)}, bf16[4,128,1024]{2,1,0:T(8,128)(2,1)}, u32[]{:S(2)}) copy-start(bf16[4,128,1024]{2,1,0:T(8,128)(2,1)} %param.20) | copy-start | bytes 3145732
  83.3 7.0 %copy-start.26 = (f32[1024]{0:T(1024)S(1)}, f32[1024]{0:T(1024)}, u32[]{:S(2)}) copy-start(f32[1024]{0:T(1024)} %param.21) | copy-start | bytes 12292
  83.3 23.8 %collective-permute-start.15 = (bf16[256,4096]{1,0:T(8,128)(2,1)}, bf16[256,4096]{1,0:T(8,128)(2,1)}, u32[]{:S(2)}, u32[]{:S(2)}) collective-permute-start(bf16[256,4096]{1,0:T(8,128)(2,1)} %shard_map.114), channel_id=1, source_target_pairs={{0,8},{8,0},{16,24},{24,16},{32,40},{40,32},{48,56},{56,48},{64,72... | collective-permute-start | bytes 6291464 | tf_op jit(solution)/shard_map/ppermute | solution.py:25
  85.9 17.6 %copy-start.10 = (bf16[64,4096]{1,0:T(8,128)(2,1)}, bf16[64,4096]{1,0:T(8,128)(2,1)S(1)}, u32[]{:S(2)}) copy-start(bf16[64,4096]{1,0:T(8,128)(2,1)S(1)} %collective-permute-done.12.refs_2_.refs_14_.refs_4_) | copy-start | bytes 1572868
  87.4 19.7 %collective-permute-start.16 = (bf16[192,4096]{1,0:T(8,128)(2,1)}, bf16[192,4096]{1,0:T(8,128)(2,1)}, u32[]{:S(2)}, u32[]{:S(2)}) collective-permute-start(bf16[192,4096]{1,0:T(8,128)(2,1)} %shard_map.115), channel_id=1, source_target_pairs={{0,8},{8,0},{16,24},{24,16},{32,40},{40,32},{48,56},{56,48},{64,72... | collective-permute-start | bytes 4718600 | tf_op jit(solution)/shard_map/ppermute | solution.py:25
  89.0 13.7 %collective-permute-start.13 = (bf16[64,4096]{1,0:T(8,128)(2,1)S(1)}, bf16[64,4096]{1,0:T(8,128)(2,1)}, u32[]{:S(2)}, u32[]{:S(2)}) collective-permute-start(bf16[64,4096]{1,0:T(8,128)(2,1)S(1)} %copy-done.4), channel_id=1, source_target_pairs={{0,48},{8,56},{16,0},{24,8},{32,16},{40,24},{48,32},{56,40},{64,11... | collective-permute-start | bytes 1572872 | tf_op jit(solution)/shard_map/ppermute | solution.py:25
  92.3 25.1 %all-to-all-start.1 = ((bf16[8,528,128]{2,1,0:T(8,128)(2,1)}), bf16[8,528,128]{2,1,0:T(8,128)(2,1)}, u32[]{:S(2)}, u32[]{:S(2)}) async-start(bf16[8,528,128]{2,1,0:T(8,128)(2,1)} %copy-done.5), calls=%async_computation.1 | async-start | bytes 2162688 | tf_op jit(solution)/shard_map/all_to_all | solution.py:428
  96.6 11.3 %copy-start.16 = (bf16[512,512]{1,0:T(8,128)(2,1)S(1)}, bf16[512,512]{1,0:T(8,128)(2,1)}, u32[]{:S(2)}) copy-start(bf16[512,512]{1,0:T(8,128)(2,1)} %copy-done.14) | copy-start | bytes 1572868
  96.6 11.3 %copy-start.20 = (bf16[512,512]{1,0:T(8,128)(2,1)S(1)}, bf16[512,512]{1,0:T(8,128)(2,1)}, u32[]{:S(2)}) copy-start(bf16[512,512]{1,0:T(8,128)(2,1)} %copy-done.19) | copy-start | bytes 1572868
  102.7 4.4 %collective-permute-start.17 = (bf16[64,4096]{1,0:T(8,128)(2,1)}, bf16[64,4096]{1,0:T(8,128)(2,1)S(1)}, u32[]{:S(2)}, u32[]{:S(2)}) collective-permute-start(bf16[64,4096]{1,0:T(8,128)(2,1)} %collective-permute-done.13.refs_15_), channel_id=1, source_target_pairs={{0,8},{8,0},{16,24},{24,16},{32,40},{40,32},{48,56},{56,48},{64,72... | collective-permute-start | bytes 1572872 | tf_op jit(solution)/shard_map/ppermute | solution.py:25
  104.4 17.2 %collective-permute-start.18 = (bf16[128,2048]{1,0:T(8,128)(2,1)}, bf16[128,2048]{1,0:T(8,128)(2,1)S(1)}, u32[]{:S(2)}, u32[]{:S(2)}) collective-permute-start(bf16[128,2048]{1,0:T(8,128)(2,1)} %shard_map.119.refs_0_), channel_id=1, source_target_pairs={{0,16},{8,24},{16,32},{24,40},{32,48},{40,56},{48,0},{56,8},{64,80... | collective-permute-start | bytes 1572872 | tf_op jit(solution)/shard_map/ppermute | solution.py:25
  104.4 17.2 %collective-permute-start.19 = (bf16[128,2048]{1,0:T(8,128)(2,1)}, bf16[128,2048]{1,0:T(8,128)(2,1)S(1)}, u32[]{:S(2)}, u32[]{:S(2)}) collective-permute-start(bf16[128,2048]{1,0:T(8,128)(2,1)} %shard_map.119.refs_0_), channel_id=1, source_target_pairs={{0,48},{8,56},{16,0},{24,8},{32,16},{40,24},{48,32},{56,40},{64,11... | collective-permute-start | bytes 1572872 | tf_op jit(solution)/shard_map/ppermute | solution.py:25
  121.6 17.9 %copy-start.6 = (bf16[512,1024]{1,0:T(8,128)(2,1)}, bf16[512,1024]{1,0:T(8,128)(2,1)S(1)}, u32[]{:S(2)}) copy-start(bf16[512,1024]{1,0:T(8,128)(2,1)S(1)} %get-tuple-element.11.refs_3_.refs_2_.hidden_ref) | copy-start | bytes 3145732
  124.0 15.4 %collective-permute-start.22 = (bf16[384,2048]{1,0:T(8,128)(2,1)}, bf16[384,2048]{1,0:T(8,128)(2,1)}, u32[]{:S(2)}, u32[]{:S(2)}) collective-permute-start(bf16[384,2048]{1,0:T(8,128)(2,1)} %shard_map.120), channel_id=1, source_target_pairs={{0,8},{8,0},{16,24},{24,16},{32,40},{40,32},{48,56},{56,48},{64,72... | collective-permute-start | bytes 4718600 | tf_op jit(solution)/shard_map/ppermute | solution.py:25
  124.6 9.2 %collective-permute-start.20 = (bf16[64,2048]{1,0:T(8,128)(2,1)S(1)}, bf16[64,2048]{1,0:T(8,128)(2,1)S(1)}, u32[]{:S(2)}, u32[]{:S(2)}) collective-permute-start(bf16[64,2048]{1,0:T(8,128)(2,1)S(1)} %slice.32), channel_id=1, source_target_pairs={{0,16},{8,24},{16,32},{24,40},{32,48},{40,56},{48,0},{56,8},{64,80... | collective-permute-start | bytes 786440 | tf_op jit(solution)/shard_map/ppermute | solution.py:25
  124.7 9.1 %collective-permute-start.21 = (bf16[64,2048]{1,0:T(8,128)(2,1)S(1)}, bf16[64,2048]{1,0:T(8,128)(2,1)S(1)}, u32[]{:S(2)}, u32[]{:S(2)}) collective-permute-start(bf16[64,2048]{1,0:T(8,128)(2,1)S(1)} %slice.33), channel_id=1, source_target_pairs={{0,48},{8,56},{16,0},{24,8},{32,16},{40,24},{48,32},{56,40},{64,11... | collective-permute-start | bytes 786440 | tf_op jit(solution)/shard_map/ppermute | solution.py:25
  134.8 4.7 %collective-permute-start.23 = (bf16[128,2048]{1,0:T(8,128)(2,1)}, bf16[128,2048]{1,0:T(8,128)(2,1)}, u32[]{:S(2)}, u32[]{:S(2)}) collective-permute-start(bf16[128,2048]{1,0:T(8,128)(2,1)} %shard_map.121), channel_id=1, source_target_pairs={{0,8},{8,0},{16,24},{24,16},{32,40},{40,32},{48,56},{56,48},{64,72... | collective-permute-start | bytes 1572872 | tf_op jit(solution)/shard_map/ppermute | solution.py:25
  136.5 15.0 %collective-permute-start.24 = (bf16[128,2048]{1,0:T(8,128)(2,1)}, bf16[128,2048]{1,0:T(8,128)(2,1)S(1)}, u32[]{:S(2)}, u32[]{:S(2)}) collective-permute-start(bf16[128,2048]{1,0:T(8,128)(2,1)} %shard_map.123.refs_0_), channel_id=1, source_target_pairs={{0,16},{8,24},{16,32},{24,40},{32,48},{40,56},{48,0},{56,8},{64,80... | collective-permute-start | bytes 1572872 | tf_op jit(solution)/shard_map/ppermute | solution.py:25
  136.5 15.0 %collective-permute-start.25 = (bf16[128,2048]{1,0:T(8,128)(2,1)}, bf16[128,2048]{1,0:T(8,128)(2,1)}, u32[]{:S(2)}, u32[]{:S(2)}) collective-permute-start(bf16[128,2048]{1,0:T(8,128)(2,1)} %shard_map.123.refs_0_), channel_id=1, source_target_pairs={{0,48},{8,56},{16,0},{24,8},{32,16},{40,24},{48,32},{56,40},{64,11... | collective-permute-start | bytes 1572872 | tf_op jit(solution)/shard_map/ppermute | solution.py:25
  146.5 32.4 %all-to-all-start.2 = ((bf16[8,528,256]{2,1,0:T(8,128)(2,1)}), bf16[8,528,256]{2,1,0:T(8,128)(2,1)}, u32[]{:S(2)}, u32[]{:S(2)}) async-start(bf16[8,528,256]{2,1,0:T(8,128)(2,1)} %shard_map.122.refs_3_.refs_2_), calls=%async_computation.2 | async-start | bytes 4325376 | tf_op jit(solution)/shard_map/all_to_all | solution.py:481
  152.8 13.5 %copy-start.7 = (bf16[512,1024]{1,0:T(8,128)(2,1)S(1)}, bf16[512,1024]{1,0:T(8,128)(2,1)}, u32[]{:S(2)}) copy-start(bf16[512,1024]{1,0:T(8,128)(2,1)} %copy-done.6) | copy-start | bytes 3145732
  152.9 13.5 %collective-permute-start.28 = (bf16[384,2048]{1,0:T(8,128)(2,1)S(1)}, bf16[384,2048]{1,0:T(8,128)(2,1)S(1)}, u32[]{:S(2)}, u32[]{:S(2)}) collective-permute-start(bf16[384,2048]{1,0:T(8,128)(2,1)S(1)} %shard_map.124), channel_id=1, source_target_pairs={{0,8},{8,0},{16,24},{24,16},{32,40},{40,32},{48,56},{56,48},{64,72... | collective-permute-start | bytes 4718600 | tf_op jit(solution)/shard_map/ppermute | solution.py:25
  153.7 9.6 %collective-permute-start.26 = (bf16[64,2048]{1,0:T(8,128)(2,1)S(1)}, bf16[64,2048]{1,0:T(8,128)(2,1)S(1)}, u32[]{:S(2)}, u32[]{:S(2)}) collective-permute-start(bf16[64,2048]{1,0:T(8,128)(2,1)S(1)} %slice.37), channel_id=1, source_target_pairs={{0,16},{8,24},{16,32},{24,40},{32,48},{40,56},{48,0},{56,8},{64,80... | collective-permute-start | bytes 786440 | tf_op jit(solution)/shard_map/ppermute | solution.py:25
  155.7 7.8 %collective-permute-start.27 = (bf16[64,2048]{1,0:T(8,128)(2,1)S(1)}, bf16[64,2048]{1,0:T(8,128)(2,1)S(1)}, u32[]{:S(2)}, u32[]{:S(2)}) collective-permute-start(bf16[64,2048]{1,0:T(8,128)(2,1)S(1)} %slice.38), channel_id=1, source_target_pairs={{0,48},{8,56},{16,0},{24,8},{32,16},{40,24},{48,32},{56,40},{64,11... | collective-permute-start | bytes 786440 | tf_op jit(solution)/shard_map/ppermute | solution.py:25
  163.7 2.6 %collective-permute-start.29 = (bf16[128,2048]{1,0:T(8,128)(2,1)S(1)}, bf16[128,2048]{1,0:T(8,128)(2,1)S(1)}, u32[]{:S(2)}, u32[]{:S(2)}) collective-permute-start(bf16[128,2048]{1,0:T(8,128)(2,1)S(1)} %shard_map.125), channel_id=1, source_target_pairs={{0,8},{8,0},{16,24},{24,16},{32,40},{40,32},{48,56},{56,48},{64,72... | collective-permute-start | bytes 1572872 | tf_op jit(solution)/shard_map/ppermute | solution.py:25
  178.9 34.5 %all-to-all-start.3 = ((bf16[8,512,256]{2,1,0:T(8,128)(2,1)}), bf16[8,512,256]{2,1,0:T(8,128)(2,1)S(1)}, u32[]{:S(2)}, u32[]{:S(2)}) async-start(bf16[8,512,256]{2,1,0:T(8,128)(2,1)} %shard_map.126), calls=%async_computation.3 | async-start | bytes 4194304 | tf_op jit(solution)/shard_map/all_to_all | solution.py:481
  (15 other events, 28.2 us)

commit v2 on v1

--- a/solution.py
+++ b/solution.py
@@ -45,36 +45,43 @@
 
 def concat(pieces, gates=()):
     cols = pieces[0][0].shape[-1]
-    grid = 2 if cols > 512 else 1
-    wide = cols // grid
-    counts, specs = [], []
+    counts = []
     for a, at in pieces:
-        if at is None:
-            counts.append(a.shape[0])
-            specs.append(pl.BlockSpec((a.shape[0], wide), lambda i: (0, i)))
+        if isinstance(at, tuple):
+            counts.append(at[1])
         else:
-            counts.append(a.shape[1])
-            specs.append(
-                pl.BlockSpec((1, a.shape[1], wide), functools.partial(lambda n, i: (n, 0, i), at))
-            )
+            counts.append(a.shape[0] if at is None else a.shape[1])
     total = sum(counts)
 
     def kernel(*refs):
-        out = refs[-1]
+        out, sems = refs[-2], refs[-1]
         row = 0
-        for ref, (_, at), count in zip(refs, pieces, counts):
-            out[row : row + count, :] = ref[...] if at is None else ref[0]
+        copies = []
+        for n, (ref, (_, at), count) in enumerate(zip(refs, pieces, counts)):
+            if isinstance(at, tuple):
+                ref = ref.at[pl.ds(at[0], count)]
+            elif at is not None:
+                ref = ref.at[at]
+            copies.append(pltpu.make_async_copy(ref, out.at[pl.ds(row, count)], sems.at[n]))
             row += count
+        load_all(copies)
 
     return pl.pallas_call(
         kernel,
         out_shape=jax.ShapeDtypeStruct((total, cols), bf16),
-        grid=(grid,),
-        in_specs=specs + [ANY] * len(gates),
-        out_specs=pl.BlockSpec((total, wide), lambda i: (0, i)),
+        in_specs=[ANY] * len(pieces) + [ANY] * len(gates),
+        out_specs=pl.BlockSpec(memory_space=pltpu.VMEM),
+        scratch_shapes=[pltpu.SemaphoreType.DMA((len(pieces),))],
         compiler_params=LIMIT,
         cost_estimate=cost(total * cols / 2**18),
     )(*[a for a, _ in pieces], *gates)
+
+
+def load_all(copies):
+    for copy in copies:
+        copy.start()
+    for copy in copies:
+        copy.wait()
 
 
 def fence(values, gates=()):
@@ -463,8 +470,8 @@
         left = move_rep(own, dx=1)
         right = move_rep(own, dx=-1)
         gates = (left, right)
-        far_a = move_rep(left[:64], dx=1)
-        far_b = move_rep(right[64:], dx=-1)
+        far_a = move_rep(concat([(left, (0, 64))]), dx=1)
+        far_b = move_rep(concat([(right, (64, 64))]), dx=-1)
         near = concat([(v, None) for v in (own, left, right)], (before,))
         far = concat([(v, None) for v in (far_a, far_b)], (before,))
         weights = [

time: 216 us -> 214 us (level)
  starting transfers between devices: 65.8 us -> 62.9 us
    all_to_all x2, starting transfers between devices: 12 us -> 9.05 us  [per_device(): sums.append(lax.all_to_all(partial, 'tp', 0, 0, tiled=True))]
    unnamed x61 -> x63, local copies, waits for them, and re-layouts: 11.2 us -> 12.4 us
    pallas_call x9 -> x13, Pallas kernels: 10.7 us -> 9.82 us  [concat(): pl.pallas_call(kernel, out_shape=jax.ShapeDtypeStruct((total, cols), bf16...]
  transfers between devices with their start and end apart: 34 -> 34, of which waited for: 14 -> 12; matrix products, arithmetic and copies ran while one was open for 2% -> 1% of each run, Pallas kernels for 15% -> 15%
where the time goes in v2:
time: 214 us; the launch traced here: 213 us
  waiting for transfers between devices  95.3 us (45%)
  starting transfers between devices  62.9 us (29%)
  Pallas kernels  37.9 us (18%)
  local copies, waits for them, and re-layouts  12.4 us (6%)
  other arithmetic  3.49 us (2%)
    all_to_all x2, waiting for transfers between devices, per_device(): sums.append(lax.all_to_all(partial, 'tp', 0, 0, tiled=True))  33.5 us
    ppermute x23, starting transfers between devices, move_rep(): return lax.ppermute(v, 'rep', perm)  33.2 us
    ppermute x23, waiting for transfers between devices, move_rep(): return lax.ppermute(v, 'rep', perm)  31.9 us
    ppermute x7, waiting for transfers between devices, move_tp(): return lax.ppermute(v, 'tp', perm)  30 us
    unnamed x63, local copies, waits for them, and re-layouts  12.4 us
    ppermute x7, starting transfers between devices, move_tp(): return lax.ppermute(v, 'tp', perm)  9.88 us
    pallas_call x13, Pallas kernels, concat(): pl.pallas_call(kernel, out_shape=jax.ShapeDtypeStruct((total, cols), bf16...  9.82 us
    pallas_call x2, Pallas kernels, query_product(): pl.pallas_call(kernel, out_shape=jax.ShapeDtypeStruct((8, rows + tail, w)...  9.6 us
  transfers between devices with their start and end apart: 34, of which 12 were waited for; matrix products, arithmetic and copies ran while one was open for 1% of the time, Pallas kernels for 15%

profile of v2, /device:TPU:1, one launch (start us, length us, event | category | flops | bytes accessed | tf_op | source)
XLA Modules:
  0.0 212.7 jit_solution(16252559703643956638)
XLA Ops:
  0.1 2.7 %shard_map.109.refs_1_ = bf16[8,64,1024]{2,1,0:T(8,128)(2,1)} custom-call(s32[2]{0:T(128)S(1)} %pad_add_fusion.ids_ref, bf16[512,8192]{1,0:T(8,128)(2,1)} %out_held_ref.1, bf16[8192,512]{1,0:T(8,128)(2,1)} %query_held_ref.1), custom_call_target="tpu_custom_call" | custom-call | bytes 2097152 | tf_op jit(solution)/shard_map/pallas_call | solution.py:106
  2.8 6.5 %all-to-all-start = ((bf16[8,64,1024]{2,1,0:T(8,128)(2,1)}), bf16[8,64,1024]{2,1,0:T(8,128)(2,1)S(1)}, u32[]{:S(2)}, u32[]{:S(2)}) async-start(bf16[8,64,1024]{2,1,0:T(8,128)(2,1)} %shard_map.109.refs_1_), calls=%async_computation | async-start | bytes 2097152 | tf_op jit(solution)/shard_map/all_to_all | solution.py:413
  9.4 1.5 collective-permute-start
  11.0 1.2 collective-permute-start.1
  12.1 1.5 collective-permute-start.3
  14.4 19.0 %collective-permute-done.rest_0_.refs_1_ = bf16[512,512]{1,0:T(8,128)(2,1)} collective-permute-done((bf16[512,512]{1,0:T(8,128)(2,1)S(1)}, bf16[512,512]{1,0:T(8,128)(2,1)}, u32[]{:S(2)}, u32[]{:S(2)}) %collective-permute-start) | collective-permute-done | bytes 524320 | tf_op jit(solution)/shard_map/ppermute | solution.py:33
  33.4 2.2 %collective-permute-done.1.rest_1_.refs_2_ = bf16[512,512]{1,0:T(8,128)(2,1)} collective-permute-done((bf16[512,512]{1,0:T(8,128)(2,1)S(1)}, bf16[512,512]{1,0:T(8,128)(2,1)}, u32[]{:S(2)}, u32[]{:S(2)}) %collective-permute-start.1) | collective-permute-done | bytes 524320 | tf_op jit(solution)/shard_map/ppermute | solution.py:33
  37.5 1.2 shard_map.111.rest_0_.refs_0_.refs_8_
  38.7 3.4 %collective-permute-start.7 = (bf16[64,4096]{1,0:T(8,128)(2,1)S(1)}, bf16[64,4096]{1,0:T(8,128)(2,1)}, u32[]{:S(2)}, u32[]{:S(2)}) collective-permute-start(bf16[64,4096]{1,0:T(8,128)(2,1)S(1)} %shard_map.111.rest_0_.refs_0_.refs_8_), channel_id=1, source_target_pairs={{0,64},{8,72},{16,80},{24,88},{32,96},{40,104},{48,112},{56,120},{... | collective-permute-start | bytes 1572872 | tf_op jit(solution)/shard_map/ppermute | solution.py:25
  42.1 1.5 collective-permute-start.4
  43.6 1.2 collective-permute-start.8
  44.8 8.8 %collective-permute-done.7.refs_1_.refs_9_ = bf16[64,4096]{1,0:T(8,128)(2,1)} collective-permute-done((bf16[64,4096]{1,0:T(8,128)(2,1)S(1)}, bf16[64,4096]{1,0:T(8,128)(2,1)}, u32[]{:S(2)}, u32[]{:S(2)}) %collective-permute-start.7) | collective-permute-done | bytes 524320 | tf_op jit(solution)/shard_map/ppermute | solution.py:25
  53.6 2.5 %collective-permute-start.9 = (bf16[64,4096]{1,0:T(8,128)(2,1)}, bf16[64,4096]{1,0:T(8,128)(2,1)S(1)}, u32[]{:S(2)}, u32[]{:S(2)}) collective-permute-start(bf16[64,4096]{1,0:T(8,128)(2,1)} %collective-permute-done.7.refs_1_.refs_9_), channel_id=1, source_target_pairs={{0,48},{8,56},{16,0},{24,8},{32,16},{40,24},{48,32},{56,40},{64,11... | collective-permute-start | bytes 1572872 | tf_op jit(solution)/shard_map/ppermute | solution.py:25
  56.3 1.2 copy-done.13
  58.6 1.4 shard_map.113.refs_0_
  60.0 1.9 collective-permute-start.5
  61.9 2.7 %collective-permute-start.11 = (bf16[64,4096]{1,0:T(8,128)(2,1)S(1)}, bf16[64,4096]{1,0:T(8,128)(2,1)}, u32[]{:S(2)}, u32[]{:S(2)}) collective-permute-start(bf16[64,4096]{1,0:T(8,128)(2,1)S(1)} %shard_map.111.rest_0_.refs_0_.refs_8_), channel_id=1, source_target_pairs={{0,48},{8,56},{16,0},{24,8},{32,16},{40,24},{48,32},{56,40},{64,11... | collective-permute-start | bytes 1572872 | tf_op jit(solution)/shard_map/ppermute | solution.py:25
  64.6 1.6 collective-permute-done.9.refs_1_
  66.2 2.3 %collective-permute-start.14 = (bf16[2,64,2048]{2,1,0:T(8,128)(2,1)S(1)}, bf16[2,64,2048]{2,1,0:T(8,128)(2,1)S(1)}, u32[]{:S(2)}, u32[]{:S(2)}) collective-permute-start(bf16[2,64,2048]{2,1,0:T(8,128)(2,1)S(1)} %shard_map.113.refs_0_), channel_id=1, source_target_pairs={{0,64},{8,72},{16,80},{24,88},{32,96},{40,104},{48,112},{56,120},{... | collective-permute-start | bytes 1572872 | tf_op jit(solution)/shard_map/ppermute | solution.py:25
  69.5 2.2 %collective-permute-start.6 = (bf16[512,512]{1,0:T(8,128)(2,1)}, bf16[512,512]{1,0:T(8,128)(2,1)}, u32[]{:S(2)}, u32[]{:S(2)}) collective-permute-start(bf16[512,512]{1,0:T(8,128)(2,1)} %collective-permute-done.4.refs_6_.refs_5_), channel_id=1, source_target_pairs={{0,3},{1,0},{2,1},{3,2},{4,7},{5,4},{6,5},{7,6},{8,11},{9,8},{10,9... | collective-permute-start | bytes 1572872 | tf_op jit(solution)/shard_map/ppermute | solution.py:33
  71.9 8.8 %collective-permute-done.5.refs_4_.refs_6_ = bf16[512,512]{1,0:T(8,128)(2,1)} collective-permute-done((bf16[512,512]{1,0:T(8,128)(2,1)}, bf16[512,512]{1,0:T(8,128)(2,1)}, u32[]{:S(2)}, u32[]{:S(2)}) %collective-permute-start.5) | collective-permute-done | bytes 524320 | tf_op jit(solution)/shard_map/ppermute | solution.py:33
  80.7 2.8 %shard_map.114 = bf16[256,4096]{1,0:T(8,128)(2,1)} custom-call(bf16[64,4096]{1,0:T(8,128)(2,1)S(1)} %shard_map.111.rest_0_.refs_0_.refs_8_, bf16[64,4096]{1,0:T(8,128)(2,1)} %collective-permute-done.7.refs_1_.refs_9_, bf16[64,4096]{1,0:T(8,128)(2,1)} %get-tuple-element.9.refs_2_.refs_10_, bf16[64,4096]{1,0:T(8,128)(2,1)} %collective-permute-done.11.refs_3_.refs_12_, ...), custom_call_target="tpu_custom_call" | custom-call | bytes 4194304 | tf_op jit(solution)/shard_map/pallas_call | solution.py:69
  83.5 2.7 %collective-permute-start.15 = (bf16[256,4096]{1,0:T(8,128)(2,1)}, bf16[256,4096]{1,0:T(8,128)(2,1)}, u32[]{:S(2)}, u32[]{:S(2)}) collective-permute-start(bf16[256,4096]{1,0:T(8,128)(2,1)} %shard_map.114), channel_id=1, source_target_pairs={{0,8},{8,0},{16,24},{24,16},{32,40},{40,32},{48,56},{56,48},{64,72... | collective-permute-start | bytes 6291464 | tf_op jit(solution)/shard_map/ppermute | solution.py:25
  86.3 1.3 shard_map.115
  87.6 1.5 collective-permute-start.16
  89.0 1.2 collective-permute-start.13
  92.3 4.3 %all-to-all-start.1 = ((bf16[8,528,128]{2,1,0:T(8,128)(2,1)}), bf16[8,528,128]{2,1,0:T(8,128)(2,1)}, u32[]{:S(2)}, u32[]{:S(2)}) async-start(bf16[8,528,128]{2,1,0:T(8,128)(2,1)} %copy-done.5), calls=%async_computation.1 | async-start | bytes 2162688 | tf_op jit(solution)/shard_map/all_to_all | solution.py:435
  96.6 6.0 %collective-permute-done.13.refs_15_ = bf16[64,4096]{1,0:T(8,128)(2,1)} collective-permute-done((bf16[64,4096]{1,0:T(8,128)(2,1)S(1)}, bf16[64,4096]{1,0:T(8,128)(2,1)}, u32[]{:S(2)}, u32[]{:S(2)}) %collective-permute-start.13) | collective-permute-done | bytes 524320 | tf_op jit(solution)/shard_map/ppermute | solution.py:25
  104.5 2.7 %collective-permute-start.19 = (bf16[128,2048]{1,0:T(8,128)(2,1)}, bf16[128,2048]{1,0:T(8,128)(2,1)S(1)}, u32[]{:S(2)}, u32[]{:S(2)}) collective-permute-start(bf16[128,2048]{1,0:T(8,128)(2,1)} %shard_map.119.refs_0_), channel_id=1, source_target_pairs={{0,48},{8,56},{16,0},{24,8},{32,16},{40,24},{48,32},{56,40},{64,11... | collective-permute-start | bytes 1572872 | tf_op jit(solution)/shard_map/ppermute | solution.py:25
  108.0 9.5 %shard_map.116.mixture_ref = f32[512,1024]{1,0:T(8,128)} custom-call(bf16[512,512]{1,0:T(8,128)(2,1)S(1)} %copy-done.21, bf16[512,512]{1,0:T(8,128)(2,1)} %collective-permute-done.rest_0_.refs_1_, bf16[512,512]{1,0:T(8,128)(2,1)} %collective-permute-done.1.rest_1_.refs_2_, bf16[512,512]{1,0:T(8,128)(2,1)} %collective-permute-done.2.refs_5_.refs_3_, ...), custom_call_target="tpu_custom_call" | custom-call | flops 4294967296 | bytes 14680064 | tf_op jit(solution)/shard_map/pallas_call | solution.py:278
  117.5 1.6 copy-done.10
  119.1 2.7 %shard_map.118 = (bf16[512,1024]{1,0:T(8,128)(2,1)S(1)}, f32[512,128]{1,0:T(8,128)S(1)}) custom-call(s32[2]{0:T(128)S(1)} %pad_add_fusion.ids_ref, f32[512,1024]{1,0:T(8,128)S(1)} %copy-done.10, bf16[8,528,128]{2,1,0:T(8,128)(2,1)} %all-to-all-done.1.res_ref), custom_call_target="tpu_custom_call" | custom-call | bytes 4194304 | tf_op jit(solution)/shard_map/pallas_call | solution.py:317
  121.8 2.6 %shard_map.122 = bf16[384,2048]{1,0:T(8,128)(2,1)} custom-call(bf16[128,2048]{1,0:T(8,128)(2,1)} %shard_map.119.refs_0_, bf16[128,2048]{1,0:T(8,128)(2,1)S(1)} %collective-permute-done.18.refs_0_.refs_1_.refs_2_, bf16[128,2048]{1,0:T(8,128)(2,1)S(1)} %collective-permute-done.19.refs_0_.refs_2_.refs_3_, ...), custom_call_target="tpu_custom_call" | custom-call | bytes 3145728 | tf_op jit(solution)/shard_map/pallas_call | solution.py:69
  125.2 2.7 %collective-permute-start.21 = (bf16[64,2048]{1,0:T(8,128)(2,1)S(1)}, bf16[64,2048]{1,0:T(8,128)(2,1)S(1)}, u32[]{:S(2)}, u32[]{:S(2)}) collective-permute-start(bf16[64,2048]{1,0:T(8,128)(2,1)S(1)} %shard_map.121), channel_id=1, source_target_pairs={{0,48},{8,56},{16,0},{24,8},{32,16},{40,24},{48,32},{56,40},{64,11... | collective-permute-start | bytes 786440 | tf_op jit(solution)/shard_map/ppermute | solution.py:25
  127.9 6.4 %collective-permute-done.20.refs_0_.refs_3_ = bf16[64,2048]{1,0:T(8,128)(2,1)S(1)} collective-permute-done((bf16[64,2048]{1,0:T(8,128)(2,1)S(1)}, bf16[64,2048]{1,0:T(8,128)(2,1)S(1)}, u32[]{:S(2)}, u32[]{:S(2)}) %collective-permute-start.20) | collective-permute-done | bytes 262176 | tf_op jit(solution)/shard_map/ppermute | solution.py:25
  136.2 2.8 %collective-permute-start.25 = (bf16[128,2048]{1,0:T(8,128)(2,1)}, bf16[128,2048]{1,0:T(8,128)(2,1)S(1)}, u32[]{:S(2)}, u32[]{:S(2)}) collective-permute-start(bf16[128,2048]{1,0:T(8,128)(2,1)} %shard_map.125.refs_0_), channel_id=1, source_target_pairs={{0,48},{8,56},{16,0},{24,8},{32,16},{40,24},{48,32},{56,40},{64,11... | collective-permute-start | bytes 1572872 | tf_op jit(solution)/shard_map/ppermute | solution.py:25
  139.3 1.2 copy-done.7
  142.4 5.1 %shard_map.124.refs_3_.refs_2_ = bf16[8,528,256]{2,1,0:T(8,128)(2,1)} custom-call(bf16[512,1024]{1,0:T(8,128)(2,1)S(1)} %copy-done.7, bf16[128,2048]{1,0:T(8,128)(2,1)} %shard_map.119.refs_0_, bf16[128,2048]{1,0:T(8,128)(2,1)S(1)} %collective-permute-done.18.refs_0_.refs_1_.refs_2_, bf16[128,2048]{1,0:T(8,128)(2,1)S(1)} %collective-permute-done.19.refs_0_.refs_2_.refs_3_, ...), custom_call_target="tpu_custom_call" | custom-call | flops 2147483648 | bytes 8388608 | tf_op jit(solution)/shard_map/pallas_call | solution.py:368
  147.5 4.5 %all-to-all-start.2 = ((bf16[8,528,256]{2,1,0:T(8,128)(2,1)}), bf16[8,528,256]{2,1,0:T(8,128)(2,1)}, u32[]{:S(2)}, u32[]{:S(2)}) async-start(bf16[8,528,256]{2,1,0:T(8,128)(2,1)} %shard_map.124.refs_3_.refs_2_), calls=%async_computation.2 | async-start | bytes 4325376 | tf_op jit(solution)/shard_map/all_to_all | solution.py:488
  153.1 1.1 collective-permute-start.28
  154.4 2.7 %collective-permute-start.27 = (bf16[64,2048]{1,0:T(8,128)(2,1)S(1)}, bf16[64,2048]{1,0:T(8,128)(2,1)S(1)}, u32[]{:S(2)}, u32[]{:S(2)}) collective-permute-start(bf16[64,2048]{1,0:T(8,128)(2,1)S(1)} %shard_map.127), channel_id=1, source_target_pairs={{0,48},{8,56},{16,0},{24,8},{32,16},{40,24},{48,32},{56,40},{64,11... | collective-permute-start | bytes 786440 | tf_op jit(solution)/shard_map/ppermute | solution.py:25
  157.1 6.5 %collective-permute-done.26.refs_0_.refs_3_ = bf16[64,2048]{1,0:T(8,128)(2,1)S(1)} collective-permute-done((bf16[64,2048]{1,0:T(8,128)(2,1)S(1)}, bf16[64,2048]{1,0:T(8,128)(2,1)S(1)}, u32[]{:S(2)}, u32[]{:S(2)}) %collective-permute-start.26) | collective-permute-done | bytes 262176 | tf_op jit(solution)/shard_map/ppermute | solution.py:25
  164.4 1.5 collective-permute-done.29.refs_6_
  166.0 4.5 %shard_map.130 = bf16[8,512,256]{2,1,0:T(8,128)(2,1)} custom-call(bf16[512,1024]{1,0:T(8,128)(2,1)S(1)} %copy-done.8, bf16[128,2048]{1,0:T(8,128)(2,1)} %shard_map.125.refs_0_, bf16[128,2048]{1,0:T(8,128)(2,1)S(1)} %collective-permute-done.24.refs_0_.refs_1_, bf16[128,2048]{1,0:T(8,128)(2,1)S(1)} %collective-permute-done.25.refs_0_.refs_2_, ...), custom_call_target="tpu_custom_call" | custom-call | flops 2147483648 | bytes 8388608 | tf_op jit(solution)/shard_map/pallas_call | solution.py:368
  170.5 9.3 %all-to-all-done.2 = bf16[8,528,256]{2,1,0:T(8,128)(2,1)} async-done(((bf16[8,528,256]{2,1,0:T(8,128)(2,1)}), bf16[8,528,256]{2,1,0:T(8,128)(2,1)}, u32[]{:S(2)}, u32[]{:S(2)}) %all-to-all-start.2) | async-done | bytes 2162720 | tf_op jit(solution)/shard_map/all_to_all | solution.py:488
  179.8 4.5 %all-to-all-start.3 = ((bf16[8,512,256]{2,1,0:T(8,128)(2,1)}), bf16[8,512,256]{2,1,0:T(8,128)(2,1)S(1)}, u32[]{:S(2)}, u32[]{:S(2)}) async-start(bf16[8,512,256]{2,1,0:T(8,128)(2,1)} %shard_map.130), calls=%async_computation.3 | async-start | bytes 4194304 | tf_op jit(solution)/shard_map/all_to_all | solution.py:488
  185.3 1.9 convert_reduce_fusion.1
  187.2 24.2 %all-to-all-done.3 = bf16[8,512,256]{2,1,0:T(8,128)(2,1)S(1)} async-done(((bf16[8,512,256]{2,1,0:T(8,128)(2,1)}), bf16[8,512,256]{2,1,0:T(8,128)(2,1)S(1)}, u32[]{:S(2)}, u32[]{:S(2)}) %all-to-all-start.3) | async-done | bytes 2097184 | tf_op jit(solution)/shard_map/all_to_all | solution.py:488
  (120 shorter events, 18.8 us)
Async XLA Ops:
  2.8 6.5 %copy-start.18 = (bf16[4,128,512]{2,1,0:T(8,128)(2,1)S(1)}, bf16[4,128,512]{2,1,0:T(8,128)(2,1)}, u32[]{:S(2)}) copy-start(bf16[4,128,512]{2,1,0:T(8,128)(2,1)} %param.19) | copy-start | bytes 1572868
  2.8 33.6 %copy-start.12 = (f32[4096,64]{0,1:T(8,128)S(1)}, f32[4096,64]{0,1:T(8,128)}, u32[]{:S(2)}) copy-start(f32[4096,64]{0,1:T(8,128)} %param.11) | copy-start | bytes 3145732
  2.8 33.6 %copy-start.14 = (bf16[4096,64]{0,1:T(8,128)(2,1)S(1)}, bf16[4096,64]{0,1:T(8,128)(2,1)}, u32[]{:S(2)}) copy-start(bf16[4096,64]{0,1:T(8,128)(2,1)} %param.12) | copy-start | bytes 1572868
  2.8 33.6 %copy-start.26 = (s32[32,64]{1,0:T(8,128)S(1)}, s32[32,64]{1,0:T(8,128)}, u32[]{:S(2)}) copy-start(s32[32,64]{1,0:T(8,128)} %scales_ref.2) | copy-start | bytes 24580
  2.8 33.6 %all-to-all-start = ((bf16[8,64,1024]{2,1,0:T(8,128)(2,1)}), bf16[8,64,1024]{2,1,0:T(8,128)(2,1)S(1)}, u32[]{:S(2)}, u32[]{:S(2)}) async-start(bf16[8,64,1024]{2,1,0:T(8,128)(2,1)} %shard_map.109.refs_1_), calls=%async_computation | async-start | bytes 2097152 | tf_op jit(solution)/shard_map/all_to_all | solution.py:413
  9.4 24.0 %collective-permute-start = (bf16[512,512]{1,0:T(8,128)(2,1)S(1)}, bf16[512,512]{1,0:T(8,128)(2,1)}, u32[]{:S(2)}, u32[]{:S(2)}) collective-permute-start(bf16[512,512]{1,0:T(8,128)(2,1)S(1)} %shard_map.110.refs_0_), channel_id=1, source_target_pairs={{0,4},{1,5},{2,6},{3,7},{4,0},{5,1},{6,2},{7,3},{8,12},{9,13},{10,... | collective-permute-start | bytes 1572872 | tf_op jit(solution)/shard_map/ppermute | solution.py:33
  11.0 24.7 %collective-permute-start.1 = (bf16[512,512]{1,0:T(8,128)(2,1)S(1)}, bf16[512,512]{1,0:T(8,128)(2,1)}, u32[]{:S(2)}, u32[]{:S(2)}) collective-permute-start(bf16[512,512]{1,0:T(8,128)(2,1)S(1)} %shard_map.110.refs_0_), channel_id=1, source_target_pairs={{0,1},{1,2},{2,3},{3,0},{4,5},{5,6},{6,7},{7,4},{8,9},{9,10},{10,1... | collective-permute-start | bytes 1572872 | tf_op jit(solution)/shard_map/ppermute | solution.py:33
  12.1 23.5 %collective-permute-start.3 = (bf16[512,512]{1,0:T(8,128)(2,1)S(1)}, bf16[512,512]{1,0:T(8,128)(2,1)S(1)}, u32[]{:S(2)}, u32[]{:S(2)}) collective-permute-start(bf16[512,512]{1,0:T(8,128)(2,1)S(1)} %shard_map.110.refs_0_), channel_id=1, source_target_pairs={{0,3},{1,0},{2,1},{3,2},{4,7},{5,4},{6,5},{7,6},{8,11},{9,8},{10,9... | collective-permute-start | bytes 1572872 | tf_op jit(solution)/shard_map/ppermute | solution.py:33
  37.5 18.6 %copy-start.28 = (s32[64,32]{0,1:T(8,128)S(1)}, s32[64,32]{0,1:T(8,128)}, u32[]{:S(2)}) copy-start(s32[64,32]{0,1:T(8,128)} %param.18) | copy-start | bytes 24580
  38.7 14.9 %collective-permute-start.7 = (bf16[64,4096]{1,0:T(8,128)(2,1)S(1)}, bf16[64,4096]{1,0:T(8,128)(2,1)}, u32[]{:S(2)}, u32[]{:S(2)}) collective-permute-start(bf16[64,4096]{1,0:T(8,128)(2,1)S(1)} %shard_map.111.rest_0_.refs_0_.refs_8_), channel_id=1, source_target_pairs={{0,64},{8,72},{16,80},{24,88},{32,96},{40,104},{48,112},{56,120},{... | collective-permute-start | bytes 1572872 | tf_op jit(solution)/shard_map/ppermute | solution.py:25
  42.1 18.0 %collective-permute-start.4 = (bf16[512,512]{1,0:T(8,128)(2,1)}, bf16[512,512]{1,0:T(8,128)(2,1)}, u32[]{:S(2)}, u32[]{:S(2)}) collective-permute-start(bf16[512,512]{1,0:T(8,128)(2,1)} %collective-permute-done.rest_0_.refs_1_), channel_id=1, source_target_pairs={{0,3},{1,0},{2,1},{3,2},{4,7},{5,4},{6,5},{7,6},{8,11},{9,8},{10,9... | collective-permute-start | bytes 1572872 | tf_op jit(solution)/shard_map/ppermute | solution.py:33
  43.6 18.3 %collective-permute-start.8 = (bf16[64,4096]{1,0:T(8,128)(2,1)S(1)}, bf16[64,4096]{1,0:T(8,128)(2,1)}, u32[]{:S(2)}, u32[]{:S(2)}) collective-permute-start(bf16[64,4096]{1,0:T(8,128)(2,1)S(1)} %shard_map.111.rest_0_.refs_0_.refs_8_), channel_id=1, source_target_pairs={{0,16},{8,24},{16,32},{24,40},{32,48},{40,56},{48,0},{56,8},{64,80... | collective-permute-start | bytes 1572872 | tf_op jit(solution)/shard_map/ppermute | solution.py:25
  53.6 12.6 %collective-permute-start.9 = (bf16[64,4096]{1,0:T(8,128)(2,1)}, bf16[64,4096]{1,0:T(8,128)(2,1)S(1)}, u32[]{:S(2)}, u32[]{:S(2)}) collective-permute-start(bf16[64,4096]{1,0:T(8,128)(2,1)} %collective-permute-done.7.refs_1_.refs_9_), channel_id=1, source_target_pairs={{0,48},{8,56},{16,0},{24,8},{32,16},{40,24},{48,32},{56,40},{64,11... | collective-permute-start | bytes 1572872 | tf_op jit(solution)/shard_map/ppermute | solution.py:25
  56.2 15.6 %collective-permute-start.2 = (bf16[512,512]{1,0:T(8,128)(2,1)}, bf16[512,512]{1,0:T(8,128)(2,1)}, u32[]{:S(2)}, u32[]{:S(2)}) collective-permute-start(bf16[512,512]{1,0:T(8,128)(2,1)} %collective-permute-done.rest_0_.refs_1_), channel_id=1, source_target_pairs={{0,1},{1,2},{2,3},{3,0},{4,5},{5,6},{6,7},{7,4},{8,9},{9,10},{10,1... | collective-permute-start | bytes 1572872 | tf_op jit(solution)/shard_map/ppermute | solution.py:33
  56.2 13.3 %collective-permute-start.10 = (bf16[64,4096]{1,0:T(8,128)(2,1)}, bf16[64,4096]{1,0:T(8,128)(2,1)S(1)}, u32[]{:S(2)}, u32[]{:S(2)}) collective-permute-start(bf16[64,4096]{1,0:T(8,128)(2,1)} %collective-permute-done.7.refs_1_.refs_9_), channel_id=1, source_target_pairs={{0,16},{8,24},{16,32},{24,40},{32,48},{40,56},{48,0},{56,8},{64,80... | collective-permute-start | bytes 1572872 | tf_op jit(solution)/shard_map/ppermute | solution.py:25
  60.0 20.7 %collective-permute-start.5 = (bf16[512,512]{1,0:T(8,128)(2,1)}, bf16[512,512]{1,0:T(8,128)(2,1)}, u32[]{:S(2)}, u32[]{:S(2)}) collective-permute-start(bf16[512,512]{1,0:T(8,128)(2,1)} %collective-permute-done.1.rest_1_.refs_2_), channel_id=1, source_target_pairs={{0,1},{1,2},{2,3},{3,0},{4,5},{5,6},{6,7},{7,4},{8,9},{9,10},{10,1... | collective-permute-start | bytes 1572872 | tf_op jit(solution)/shard_map/ppermute | solution.py:33
  61.9 18.8 %collective-permute-start.11 = (bf16[64,4096]{1,0:T(8,128)(2,1)S(1)}, bf16[64,4096]{1,0:T(8,128)(2,1)}, u32[]{:S(2)}, u32[]{:S(2)}) collective-permute-start(bf16[64,4096]{1,0:T(8,128)(2,1)S(1)} %shard_map.111.rest_0_.refs_0_.refs_8_), channel_id=1, source_target_pairs={{0,48},{8,56},{16,0},{24,8},{32,16},{40,24},{48,32},{56,40},{64,11... | collective-permute-start | bytes 1572872 | tf_op jit(solution)/shard_map/ppermute | solution.py:25
  66.2 14.5 %collective-permute-start.14 = (bf16[2,64,2048]{2,1,0:T(8,128)(2,1)S(1)}, bf16[2,64,2048]{2,1,0:T(8,128)(2,1)S(1)}, u32[]{:S(2)}, u32[]{:S(2)}) collective-permute-start(bf16[2,64,2048]{2,1,0:T(8,128)(2,1)S(1)} %shard_map.113.refs_0_), channel_id=1, source_target_pairs={{0,64},{8,72},{16,80},{24,88},{32,96},{40,104},{48,112},{56,120},{... | collective-permute-start | bytes 1572872 | tf_op jit(solution)/shard_map/ppermute | solution.py:25
  69.5 16.7 %collective-permute-start.6 = (bf16[512,512]{1,0:T(8,128)(2,1)}, bf16[512,512]{1,0:T(8,128)(2,1)}, u32[]{:S(2)}, u32[]{:S(2)}) collective-permute-start(bf16[512,512]{1,0:T(8,128)(2,1)} %collective-permute-done.4.refs_6_.refs_5_), channel_id=1, source_target_pairs={{0,3},{1,0},{2,1},{3,2},{4,7},{5,4},{6,5},{7,6},{8,11},{9,8},{10,9... | collective-permute-start | bytes 1572872 | tf_op jit(solution)/shard_map/ppermute | solution.py:33
  71.8 14.5 %copy-start.2 = (bf16[64,4096]{1,0:T(8,128)(2,1)S(1)}, bf16[64,4096]{1,0:T(8,128)(2,1)}, u32[]{:S(2)}) copy-start(bf16[64,4096]{1,0:T(8,128)(2,1)} %copy-done.1) | copy-start | bytes 1572868
  71.8 14.5 %copy-start.4 = (bf16[64,4096]{1,0:T(8,128)(2,1)S(1)}, bf16[64,4096]{1,0:T(8,128)(2,1)}, u32[]{:S(2)}) copy-start(bf16[64,4096]{1,0:T(8,128)(2,1)} %get-tuple-element.10.refs_1_.refs_13_.refs_3_) | copy-start | bytes 1572868
  71.8 14.4 %collective-permute-start.12 = (bf16[64,4096]{1,0:T(8,128)(2,1)}, bf16[64,4096]{1,0:T(8,128)(2,1)S(1)}, u32[]{:S(2)}, u32[]{:S(2)}) collective-permute-start(bf16[64,4096]{1,0:T(8,128)(2,1)} %get-tuple-element.9.refs_2_.refs_10_), channel_id=1, source_target_pairs={{0,16},{8,24},{16,32},{24,40},{32,48},{40,56},{48,0},{56,8},{64,80... | collective-permute-start | bytes 1572872 | tf_op jit(solution)/shard_map/ppermute | solution.py:25
  83.5 6.8 %copy-start.9 = (bf16[4,128,1024]{2,1,0:T(8,128)(2,1)S(1)}, bf16[4,128,1024]{2,1,0:T(8,128)(2,1)}, u32[]{:S(2)}) copy-start(bf16[4,128,1024]{2,1,0:T(8,128)(2,1)} %param.20) | copy-start | bytes 3145732
  83.5 6.8 %copy-start.27 = (f32[1024]{0:T(1024)S(1)}, f32[1024]{0:T(1024)}, u32[]{:S(2)}) copy-start(f32[1024]{0:T(1024)} %param.21) | copy-start | bytes 12292
  83.5 23.6 %collective-permute-start.15 = (bf16[256,4096]{1,0:T(8,128)(2,1)}, bf16[256,4096]{1,0:T(8,128)(2,1)}, u32[]{:S(2)}, u32[]{:S(2)}) collective-permute-start(bf16[256,4096]{1,0:T(8,128)(2,1)} %shard_map.114), channel_id=1, source_target_pairs={{0,8},{8,0},{16,24},{24,16},{32,40},{40,32},{48,56},{56,48},{64,72... | collective-permute-start | bytes 6291464 | tf_op jit(solution)/shard_map/ppermute | solution.py:25
  86.2 17.3 %copy-start.11 = (bf16[64,4096]{1,0:T(8,128)(2,1)}, bf16[64,4096]{1,0:T(8,128)(2,1)S(1)}, u32[]{:S(2)}) copy-start(bf16[64,4096]{1,0:T(8,128)(2,1)S(1)} %collective-permute-done.12.refs_2_.refs_14_.refs_4_) | copy-start | bytes 1572868
  87.6 19.6 %collective-permute-start.16 = (bf16[192,4096]{1,0:T(8,128)(2,1)}, bf16[192,4096]{1,0:T(8,128)(2,1)}, u32[]{:S(2)}, u32[]{:S(2)}) collective-permute-start(bf16[192,4096]{1,0:T(8,128)(2,1)} %shard_map.115), channel_id=1, source_target_pairs={{0,8},{8,0},{16,24},{24,16},{32,40},{40,32},{48,56},{56,48},{64,72... | collective-permute-start | bytes 4718600 | tf_op jit(solution)/shard_map/ppermute | solution.py:25
  89.0 13.6 %collective-permute-start.13 = (bf16[64,4096]{1,0:T(8,128)(2,1)S(1)}, bf16[64,4096]{1,0:T(8,128)(2,1)}, u32[]{:S(2)}, u32[]{:S(2)}) collective-permute-start(bf16[64,4096]{1,0:T(8,128)(2,1)S(1)} %copy-done.4), channel_id=1, source_target_pairs={{0,48},{8,56},{16,0},{24,8},{32,16},{40,24},{48,32},{56,40},{64,11... | collective-permute-start | bytes 1572872 | tf_op jit(solution)/shard_map/ppermute | solution.py:25
  92.3 25.2 %all-to-all-start.1 = ((bf16[8,528,128]{2,1,0:T(8,128)(2,1)}), bf16[8,528,128]{2,1,0:T(8,128)(2,1)}, u32[]{:S(2)}, u32[]{:S(2)}) async-start(bf16[8,528,128]{2,1,0:T(8,128)(2,1)} %copy-done.5), calls=%async_computation.1 | async-start | bytes 2162688 | tf_op jit(solution)/shard_map/all_to_all | solution.py:435
  96.6 11.4 %copy-start.17 = (bf16[512,512]{1,0:T(8,128)(2,1)S(1)}, bf16[512,512]{1,0:T(8,128)(2,1)}, u32[]{:S(2)}) copy-start(bf16[512,512]{1,0:T(8,128)(2,1)} %copy-done.15) | copy-start | bytes 1572868
  96.6 11.4 %copy-start.21 = (bf16[512,512]{1,0:T(8,128)(2,1)S(1)}, bf16[512,512]{1,0:T(8,128)(2,1)}, u32[]{:S(2)}) copy-start(bf16[512,512]{1,0:T(8,128)(2,1)} %copy-done.20) | copy-start | bytes 1572868
  102.6 4.5 %collective-permute-start.17 = (bf16[64,4096]{1,0:T(8,128)(2,1)}, bf16[64,4096]{1,0:T(8,128)(2,1)S(1)}, u32[]{:S(2)}, u32[]{:S(2)}) collective-permute-start(bf16[64,4096]{1,0:T(8,128)(2,1)} %collective-permute-done.13.refs_15_), channel_id=1, source_target_pairs={{0,8},{8,0},{16,24},{24,16},{32,40},{40,32},{48,56},{56,48},{64,72... | collective-permute-start | bytes 1572872 | tf_op jit(solution)/shard_map/ppermute | solution.py:25
  104.4 17.4 %collective-permute-start.18 = (bf16[128,2048]{1,0:T(8,128)(2,1)}, bf16[128,2048]{1,0:T(8,128)(2,1)S(1)}, u32[]{:S(2)}, u32[]{:S(2)}) collective-permute-start(bf16[128,2048]{1,0:T(8,128)(2,1)} %shard_map.119.refs_0_), channel_id=1, source_target_pairs={{0,16},{8,24},{16,32},{24,40},{32,48},{40,56},{48,0},{56,8},{64,80... | collective-permute-start | bytes 1572872 | tf_op jit(solution)/shard_map/ppermute | solution.py:25
  104.5 17.3 %collective-permute-start.19 = (bf16[128,2048]{1,0:T(8,128)(2,1)}, bf16[128,2048]{1,0:T(8,128)(2,1)S(1)}, u32[]{:S(2)}, u32[]{:S(2)}) collective-permute-start(bf16[128,2048]{1,0:T(8,128)(2,1)} %shard_map.119.refs_0_), channel_id=1, source_target_pairs={{0,48},{8,56},{16,0},{24,8},{32,16},{40,24},{48,32},{56,40},{64,11... | collective-permute-start | bytes 1572872 | tf_op jit(solution)/shard_map/ppermute | solution.py:25
  121.7 12.5 %copy-start.6 = (bf16[512,1024]{1,0:T(8,128)(2,1)}, bf16[512,1024]{1,0:T(8,128)(2,1)S(1)}, u32[]{:S(2)}) copy-start(bf16[512,1024]{1,0:T(8,128)(2,1)S(1)} %get-tuple-element.11.refs_3_.refs_2_.hidden_ref) | copy-start | bytes 3145732
  124.4 14.8 %collective-permute-start.22 = (bf16[384,2048]{1,0:T(8,128)(2,1)}, bf16[384,2048]{1,0:T(8,128)(2,1)}, u32[]{:S(2)}, u32[]{:S(2)}) collective-permute-start(bf16[384,2048]{1,0:T(8,128)(2,1)} %shard_map.122), channel_id=1, source_target_pairs={{0,8},{8,0},{16,24},{24,16},{32,40},{40,32},{48,56},{56,48},{64,72... | collective-permute-start | bytes 4718600 | tf_op jit(solution)/shard_map/ppermute | solution.py:25
  125.0 9.2 %collective-permute-start.20 = (bf16[64,2048]{1,0:T(8,128)(2,1)S(1)}, bf16[64,2048]{1,0:T(8,128)(2,1)S(1)}, u32[]{:S(2)}, u32[]{:S(2)}) collective-permute-start(bf16[64,2048]{1,0:T(8,128)(2,1)S(1)} %shard_map.120), channel_id=1, source_target_pairs={{0,16},{8,24},{16,32},{24,40},{32,48},{40,56},{48,0},{56,8},{64,80... | collective-permute-start | bytes 786440 | tf_op jit(solution)/shard_map/ppermute | solution.py:25
  125.2 9.1 %collective-permute-start.21 = (bf16[64,2048]{1,0:T(8,128)(2,1)S(1)}, bf16[64,2048]{1,0:T(8,128)(2,1)S(1)}, u32[]{:S(2)}, u32[]{:S(2)}) collective-permute-start(bf16[64,2048]{1,0:T(8,128)(2,1)S(1)} %shard_map.121), channel_id=1, source_target_pairs={{0,48},{8,56},{16,0},{24,8},{32,16},{40,24},{48,32},{56,40},{64,11... | collective-permute-start | bytes 786440 | tf_op jit(solution)/shard_map/ppermute | solution.py:25
  134.3 4.9 %collective-permute-start.23 = (bf16[128,2048]{1,0:T(8,128)(2,1)S(1)}, bf16[128,2048]{1,0:T(8,128)(2,1)}, u32[]{:S(2)}, u32[]{:S(2)}) collective-permute-start(bf16[128,2048]{1,0:T(8,128)(2,1)S(1)} %shard_map.123), channel_id=1, source_target_pairs={{0,8},{8,0},{16,24},{24,16},{32,40},{40,32},{48,56},{56,48},{64,72... | collective-permute-start | bytes 1572872 | tf_op jit(solution)/shard_map/ppermute | solution.py:25
  136.1 16.0 %collective-permute-start.24 = (bf16[128,2048]{1,0:T(8,128)(2,1)}, bf16[128,2048]{1,0:T(8,128)(2,1)S(1)}, u32[]{:S(2)}, u32[]{:S(2)}) collective-permute-start(bf16[128,2048]{1,0:T(8,128)(2,1)} %shard_map.125.refs_0_), channel_id=1, source_target_pairs={{0,16},{8,24},{16,32},{24,40},{32,48},{40,56},{48,0},{56,8},{64,80... | collective-permute-start | bytes 1572872 | tf_op jit(solution)/shard_map/ppermute | solution.py:25
  136.2 15.9 %collective-permute-start.25 = (bf16[128,2048]{1,0:T(8,128)(2,1)}, bf16[128,2048]{1,0:T(8,128)(2,1)S(1)}, u32[]{:S(2)}, u32[]{:S(2)}) collective-permute-start(bf16[128,2048]{1,0:T(8,128)(2,1)} %shard_map.125.refs_0_), channel_id=1, source_target_pairs={{0,48},{8,56},{16,0},{24,8},{32,16},{40,24},{48,32},{56,40},{64,11... | collective-permute-start | bytes 1572872 | tf_op jit(solution)/shard_map/ppermute | solution.py:25
  147.5 32.3 %all-to-all-start.2 = ((bf16[8,528,256]{2,1,0:T(8,128)(2,1)}), bf16[8,528,256]{2,1,0:T(8,128)(2,1)}, u32[]{:S(2)}, u32[]{:S(2)}) async-start(bf16[8,528,256]{2,1,0:T(8,128)(2,1)} %shard_map.124.refs_3_.refs_2_), calls=%async_computation.2 | async-start | bytes 4325376 | tf_op jit(solution)/shard_map/all_to_all | solution.py:488
  153.1 12.8 %collective-permute-start.28 = (bf16[384,2048]{1,0:T(8,128)(2,1)S(1)}, bf16[384,2048]{1,0:T(8,128)(2,1)S(1)}, u32[]{:S(2)}, u32[]{:S(2)}) collective-permute-start(bf16[384,2048]{1,0:T(8,128)(2,1)S(1)} %shard_map.128), channel_id=1, source_target_pairs={{0,8},{8,0},{16,24},{24,16},{32,40},{40,32},{48,56},{56,48},{64,72... | collective-permute-start | bytes 4718600 | tf_op jit(solution)/shard_map/ppermute | solution.py:25
  154.3 11.7 %copy-start.8 = (bf16[512,1024]{1,0:T(8,128)(2,1)S(1)}, bf16[512,1024]{1,0:T(8,128)(2,1)}, u32[]{:S(2)}) copy-start(bf16[512,1024]{1,0:T(8,128)(2,1)} %copy-done.6) | copy-start | bytes 3145732
  154.3 9.3 %collective-permute-start.26 = (bf16[64,2048]{1,0:T(8,128)(2,1)S(1)}, bf16[64,2048]{1,0:T(8,128)(2,1)S(1)}, u32[]{:S(2)}, u32[]{:S(2)}) collective-permute-start(bf16[64,2048]{1,0:T(8,128)(2,1)S(1)} %shard_map.126), channel_id=1, source_target_pairs={{0,16},{8,24},{16,32},{24,40},{32,48},{40,56},{48,0},{56,8},{64,80... | collective-permute-start | bytes 786440 | tf_op jit(solution)/shard_map/ppermute | solution.py:25
  154.4 9.2 %collective-permute-start.27 = (bf16[64,2048]{1,0:T(8,128)(2,1)S(1)}, bf16[64,2048]{1,0:T(8,128)(2,1)S(1)}, u32[]{:S(2)}, u32[]{:S(2)}) collective-permute-start(bf16[64,2048]{1,0:T(8,128)(2,1)S(1)} %shard_map.127), channel_id=1, source_target_pairs={{0,48},{8,56},{16,0},{24,8},{32,16},{40,24},{48,32},{56,40},{64,11... | collective-permute-start | bytes 786440 | tf_op jit(solution)/shard_map/ppermute | solution.py:25
  163.7 2.3 %collective-permute-start.29 = (bf16[128,2048]{1,0:T(8,128)(2,1)S(1)}, bf16[128,2048]{1,0:T(8,128)(2,1)S(1)}, u32[]{:S(2)}, u32[]{:S(2)}) collective-permute-start(bf16[128,2048]{1,0:T(8,128)(2,1)S(1)} %shard_map.129), channel_id=1, source_target_pairs={{0,8},{8,0},{16,24},{24,16},{32,40},{40,32},{48,56},{56,48},{64,72... | collective-permute-start | bytes 1572872 | tf_op jit(solution)/shard_map/ppermute | solution.py:25
  179.8 31.6 %all-to-all-start.3 = ((bf16[8,512,256]{2,1,0:T(8,128)(2,1)}), bf16[8,512,256]{2,1,0:T(8,128)(2,1)S(1)}, u32[]{:S(2)}, u32[]{:S(2)}) async-start(bf16[8,512,256]{2,1,0:T(8,128)(2,1)} %shard_map.130), calls=%async_computation.3 | async-start | bytes 4194304 | tf_op jit(solution)/shard_map/all_to_all | solution.py:488
  (16 other events, 25.7 us)
